TPU v7x, 256 devices: a whole 4x4x8 slice. The times are simulated.
256 devices in a mesh: replica: 32 (over x_hi, z, core), fsdp: 8 (over x_lo, y).
Axes of the slice: x: 4 (x_hi: 2, x_lo: 2; x = x_hi * 2 + x_lo), y: 4, z: 8, core: 2. Of those that a mesh axis runs over, the one named last changes fastest.
Arguments:
- tokens: bfloat16 [163840, 4096], P(('replica', 'fsdp')), may hold values from -6 to 6
- cotangent: bfloat16 [163840, 512], P(('replica', 'fsdp')), may hold values from -6 to 6
- momentum: float32 [32, 4096, 512], P('replica', 'fsdp'), may hold values from -24 to 24
- kept_index: int32 [32, 8, 32768], P(None, None, 'fsdp'), may hold values from 0 to 63, as said below
Outputs:
- new_momentum: float32 [32, 4096, 512], P('replica', 'fsdp')
- update: float32 [4096, 512], P('fsdp')
Inputs may be any that keep to these rules, and one draw needn't show every extreme that they name: `kept_index`: for each replica and block the 8 frequencies are distinct.
All inputs are finite; a program needn't handle non-finite values.
Results may differ from a plain program's by a relative error of at most 0.0003.
Values sent between devices are 32-bit elements; how exact they have to be, the bound alone decides.
No kernel may reach another device: no remote copies, remote signals or barrier semaphores. Data moves between devices by JAX's collectives and lax.ppermute only.
A program may use at most 128 MiB of HBM per device.

v0:
```python
import math

import jax
import jax.numpy as jnp
from jax import lax
from jax.sharding import PartitionSpec as P

BLOCK = 64


momentum_decay = 0.9


def cosines(length):
    frequency = lax.broadcasted_iota(jnp.float32, (length, length), 0)
    position = lax.broadcasted_iota(jnp.float32, (length, length), 1)
    factor = jnp.where(frequency == 0.0, math.sqrt(1.0 / length), math.sqrt(2.0 / length))
    return factor * jnp.cos(math.pi * (2.0 * position + 1.0) * frequency / (2.0 * length))


def forward(weights, cosine_rows):
    length = cosine_rows.shape[0]
    blocks = weights.reshape(weights.shape[0], weights.shape[1] // length, length)
    spectra = jnp.einsum("rbn,kn->krb", blocks, cosine_rows, precision=lax.Precision.HIGHEST)
    return spectra.reshape(length, -1)


def inverse(spectra, cosine_rows, row_width):
    length = cosine_rows.shape[0]
    spectral_grid = spectra.reshape(length, -1, row_width // length)
    rebuilt = jnp.einsum("krb,kn->rbn", spectral_grid, cosine_rows, precision=lax.Precision.HIGHEST)
    return rebuilt.reshape(-1, row_width)


def densify(kept_values, chosen, length):
    frequency = lax.broadcasted_iota(jnp.int32, (length, chosen.shape[1]), 0)
    filled = jnp.zeros((length, chosen.shape[1]), jnp.float32)
    for member_slot in range(chosen.shape[0]):
        filled = filled + jnp.where(
            frequency == chosen[member_slot][None, :], kept_values[member_slot][None, :], 0.0
        )
    return filled


def select_kept(spectra, chosen):
    frequency = lax.broadcasted_iota(jnp.int32, spectra.shape, 0)
    picked = []
    for member_slot in range(chosen.shape[0]):
        picked.append(
            jnp.sum(jnp.where(frequency == chosen[member_slot][None, :], spectra, 0.0), axis=0)
        )
    return jnp.stack(picked)


def on_device(tokens, cotangent, momentum, kept_index):
    length = BLOCK
    cosine_rows = cosines(length)
    group_size = lax.axis_size("fsdp")
    replicas = lax.axis_size("replica")
    row_width = cotangent.shape[1]
    summed = lax.psum_scatter(
        lax.dot_general(
            tokens, cotangent, (((0,), (0,)), ((), ())), preferred_element_type=jnp.float32
        ),
        "fsdp",
        scatter_dimension=0,
        tiled=True,
    )
    factor = 1.0 / math.sqrt(tokens.shape[0] * group_size)
    moment = momentum_decay * momentum[0] + factor * summed
    own_chosen = lax.dynamic_index_in_dim(kept_index, lax.axis_index("replica"), 0, keepdims=False)
    spectra = forward(moment, cosine_rows)
    kept_values = select_kept(spectra, own_chosen)
    own_rebuilt = inverse(densify(kept_values, own_chosen, length), cosine_rows, row_width)
    new_momentum = moment - own_rebuilt
    piece = lax.all_gather(kept_values[None], "replica", axis=0, tiled=True)
    positions = jnp.arange(piece.shape[0], dtype=jnp.int32)

    def spread_one(member):
        chosen = lax.dynamic_index_in_dim(kept_index, member[1], 0, keepdims=False)
        return densify(member[0], chosen, length)

    filled_all = lax.map(spread_one, (piece, positions))
    update = inverse(jnp.sum(filled_all, axis=0), cosine_rows, row_width) / replicas
    return (new_momentum[None], update)


def solution(mesh):
    in_specs = (
        P(("replica", "fsdp"), None),
        P(("replica", "fsdp"), None),
        P("replica", "fsdp", None),
        P(None, None, "fsdp"),
    )
    out_specs = (P("replica", "fsdp", None), P("fsdp", None))
    return jax.shard_map(
        on_device, mesh=mesh, in_specs=in_specs, out_specs=out_specs, check_vma=False
    )
```

profile of v0, /device:TPU:1, one launch (start us, length us, event | category | flops | bytes accessed | tf_op | source)
XLA Modules:
  0.0 486.6 jit_solution(10704500592181215404)
XLA Ops:
  8.3 8.3 %fusion.65 = f32[4096,512]{1,0:T(8,128)} fusion(bf16[640,4096]{1,0:T(8,128)(2,1)} %param.6, bf16[640,512]{1,0:T(8,128)(2,1)S(1)} %copy-done), kind=kOutput, calls=%fused_computation.126 | convolution fusion | flops 2684354560 | bytes 14286848 | tf_op jit(solution)/shard_map/dot_general | solution.py:62
  17.1 2.6 fusion.58
  19.7 96.1 %reduce-scatter.2.cloned.1.call-done = f32[512,512]{1,0:T(8,128)} async-done(((f32[4096,512]{1,0:T(8,128)}), f32[512,512]{1,0:T(8,128)}) %reduce-scatter.2.cloned.1.call-update) | async-done | bytes 1048592 | tf_op jit(solution)/shard_map/reduce_scatter | solution.py:61
  119.0 5.4 %select_reduce_fusion.7 = (f32[4096]{0:T(1024)S(1)}, f32[4096]{0:T(1024)S(1)}, f32[4096]{0:T(1024)S(1)}, f32[4096]{0:T(1024)S(1)}, f32[4096]{0:T(1024)S(1)}, /*i...) fusion(s32[4096]{0:T(1024)S(1)} %bitcast.112, s32[4096]{0:T(1024)S(1)} %bitcast.118, s32[4096]{0:T(1024)S(1)} %bitcast.117, ...), kind=kOutput, calls=%fused_computation.67 | convolution fusion | flops 207597568 | bytes 1311488 | tf_op jit(solution)/shard_map/rbn,kn->krb/dot_general | solution.py:24
  129.6 3.3 fusion.5
  135.7 75.8 %all-gather.3.cloned.1.call-done = f32[256,4096]{1,0:T(8,128)} async-done(((f32[8,4096]{1,0:T(8,128)}), f32[256,4096]{1,0:T(8,128)}) %all-gather.3.cloned.1.call-update) | async-done | bytes 4194320 | tf_op jit(solution)/shard_map/all_gather | solution.py:76
  211.5 247.5 %while.10 = (s32[]{:T(128)}, f32[32,64,4096]{2,1,0:T(8,128)}, s32[32]{0:T(128)S(1)}, s32[32,8,4096]{2,1,0:T(8,128)}, f32[32,8,4096]{2,1,0:T(8,128)}, /*index=5*/...) while((s32[]{:T(128)}, f32[32,64,4096]{2,1,0:T(8,128)}, ...), condition=%wide.region_10.11_spmd, body=%wide.region_9.10_spmd.sunk | while | flops 6029324 | bytes 1835355 | solution.py:83
  229.2 1.9 constant_dynamic-slice_fusion.35
  238.6 1.9 constant_dynamic-slice_fusion.34
  244.9 1.8 constant_dynamic-slice_fusion.35
  261.8 1.9 constant_dynamic-slice_fusion.34
  275.6 1.9 constant_dynamic-slice_fusion.35
  279.2 1.9 add_dynamic-update-slice_fusion.2
  285.2 1.9 constant_dynamic-slice_fusion.34
  291.4 1.9 constant_dynamic-slice_fusion.35
  310.0 1.8 add_dynamic-update-slice_fusion.2
  331.1 1.9 constant_dynamic-slice_fusion.34
  337.4 1.9 constant_dynamic-slice_fusion.35
  345.2 1.9 constant_dynamic-slice_fusion.35
  354.8 1.9 constant_dynamic-slice_fusion.34
  370.2 1.9 constant_dynamic-slice_fusion.34
  376.3 1.9 constant_dynamic-slice_fusion.35
  391.8 1.9 constant_dynamic-slice_fusion.35
  403.0 1.9 add_dynamic-update-slice_fusion.2
  407.4 1.9 constant_dynamic-slice_fusion.35
  416.9 1.9 constant_dynamic-slice_fusion.34
  433.9 1.8 add_dynamic-update-slice_fusion.2
  445.8 1.9 constant_dynamic-slice_fusion.35
  455.3 1.8 constant_dynamic-slice_fusion.34
  458.9 12.6 %reduce_sum.89 = f32[64,4096]{1,0:T(8,128)} reduce(f32[32,64,4096]{2,1,0:T(8,128)} %get-tuple-element.29, f32[]{:T(128)} %constant.23.clone.1), dimensions={0}, to_apply=%region_11.12 | reduce | flops 8126464 | bytes 34603012 | tf_op jit(solution)/shard_map/reduce_sum | solution.py:84
  473.4 3.8 fusion.2
  477.2 2.5 copy.54
  (159 shorter events, 158.1 us)
Async XLA Ops:
  7.2 1.1 copy-start
  7.2 108.6 %reduce-scatter.2.cloned.1.call-start = ((), (), s32[]{:S(2)}) async-start(), calls=%async_computation.1 | async-start | bytes 9437184 | tf_op jit(solution)/shard_map/reduce_scatter | solution.py:61
  16.5 99.3 %copy-start.2 = (f32[1,512,512]{2,1,0:T(8,128)S(1)}, f32[1,512,512]{2,1,0:T(8,128)}, u32[]{:S(2)}) copy-start(f32[1,512,512]{2,1,0:T(8,128)} %param.8) | copy-start | bytes 3145732
  16.5 194.9 %all-gather.3.cloned.1.call-start = ((), (), s32[]{:S(2)}) async-start(), calls=%async_computation.2 | async-start | bytes 4325376 | tf_op jit(solution)/shard_map/all_gather | solution.py:76
  458.9 20.8 %copy-start.1 = (bf16[640,512]{1,0:T(8,128)(2,1)S(1)}, bf16[640,512]{1,0:T(8,128)(2,1)}, u32[]{:S(2)}) copy-start(bf16[640,512]{1,0:T(8,128)(2,1)} %param.7) | copy-start | bytes 1966084
Sparse Core Ops, SparseCore 0:
  16.7 99.0 reduce-scatter.1
  125.4 85.9 all-gather.2
where the time goes:
time: 490 us; the launch traced here: 487 us
  waiting for transfers between devices  172 us (35%)
  local copies, waits for them, and re-layouts  145 us (30%)
  other arithmetic  72.5 us (15%)
  loops' own time  62.4 us (13%)
  matrix products  20.7 us (4%)
  between operations  14.2 us (3%)
    reduce_scatter x1, waiting for transfers between devices, on_device(): lax.psum_scatter(lax.dot_general(tokens, cotangent, (((0,), (0,)), ((), (...  96.1 us
    all_gather x1, waiting for transfers between devices, on_device(): piece = lax.all_gather(kept_values[None], 'replica', axis=0, tiled=True)  75.8 us
    another operation x1, loops' own time, on_device(): filled_all = lax.map(spread_one, (piece, positions))  62.4 us
    slice x34, local copies, waits for them, and re-layouts, densify(): chosen[member_slot][None, :]  57.9 us
    dynamic_update_slice x32, other arithmetic, on_device(): filled_all = lax.map(spread_one, (piece, positions))  57.2 us
    slice x32, local copies, waits for them, and re-layouts, densify(): kept_values[member_slot][None, :]  54.4 us
    dynamic_slice x32, local copies, waits for them, and re-layouts, on_device(): filled_all = lax.map(spread_one, (piece, positions))  18.6 us
    reduce_sum x1, other arithmetic, on_device(): jnp.sum(filled_all, axis=0)  12.6 us
  transfers between devices with their start and end apart: 2, of which 2 were waited for; matrix products, arithmetic and copies ran while one was open for 3% of the time, Pallas kernels for 0%

commit v1 on v0

v1 whole, which is shorter than its diff:
```python
import functools
import math

import jax
import jax.numpy as jnp
import numpy as np
from jax import lax
from jax.experimental import pallas as pl
from jax.experimental.pallas import tpu as pltpu
from jax.sharding import PartitionSpec as P

BLOCK = 64
KEEP = 8
HALF = 256
PART = 128
DECAY = 0.9
BF16 = jnp.bfloat16
F32 = jnp.float32
VMEM = pl.BlockSpec(memory_space=pltpu.VMEM)
HBM = pl.BlockSpec(memory_space=pltpu.HBM)
SMEM = pl.BlockSpec(memory_space=pltpu.SMEM)
ANY = pl.BlockSpec(memory_space=pl.ANY)
COST = pl.CostEstimate(flops=1, bytes_accessed=1, transcendentals=0)


def paired_cosines():
    k = np.arange(BLOCK, dtype=np.float64)[:, None]
    n = np.arange(BLOCK, dtype=np.float64)[None, :]
    c = np.sqrt(np.where(k == 0, 1.0, 2.0) / BLOCK) * np.cos(np.pi * (2 * n + 1) * k / (2 * BLOCK))
    both = np.zeros((2 * BLOCK, 2 * BLOCK))
    both[:BLOCK, :BLOCK] = c
    both[BLOCK:, BLOCK:] = c
    return both.astype(np.float32)


def halves(value):
    high = value.astype(BF16)
    return high, (value - high.astype(F32)).astype(BF16)


def stacked_cosines():
    pair = paired_cosines()
    high = pair.astype(jnp.bfloat16)
    low = (pair - high.astype(np.float32)).astype(jnp.bfloat16)
    return np.concatenate([high, high, low], axis=1), np.concatenate([high, high, low], axis=0)


def products(tokens, cotangent, table, units, splits, limit, after=()):
    depth, width = cotangent.shape
    count = len(units)
    shapes = []
    for group in splits:
        if group == "parts":
            shapes += [(PART, width)] * (HALF // PART)
        else:
            shapes.append((HALF * group, width))

    def kernel(table_ref, tokens_ref, cot_ref, *refs):
        out_refs, (buffer, sems) = refs[len(after) : -2], refs[-2:]
        copies = []
        for m in range(count):
            column = pl.multiple_of(table_ref[m] * HALF, HALF)
            copies.append(pltpu.make_async_copy(tokens_ref.at[:, pl.ds(column, HALF)], buffer.at[m], sems.at[m]))
            copies[-1].start()
        at = 0
        out = 0
        for group in splits:
            for m in range(1 if group == "parts" else group):
                copies[at].wait()
                value = lax.dot_general(
                    buffer[at], cot_ref[...], (((0,), (0,)), ((), ())), preferred_element_type=F32
                )
                if group == "parts":
                    for p in range(HALF // PART):
                        out_refs[out + p][...] = value[p * PART : (p + 1) * PART]
                else:
                    out_refs[out][m * HALF : (m + 1) * HALF, :] = value
                at += 1
            out += HALF // PART if group == "parts" else 1

    return pl.pallas_call(
        kernel,
        out_shape=[jax.ShapeDtypeStruct(s, F32) for s in shapes],
        in_specs=[SMEM, HBM, VMEM] + [ANY] * len(after),
        out_specs=[VMEM] * len(shapes),
        scratch_shapes=[pltpu.VMEM((count, depth, HALF), BF16), pltpu.SemaphoreType.DMA((count,))],
        compiler_params=pltpu.CompilerParams(vmem_limit_bytes=limit),
        cost_estimate=COST,
    )(jnp.stack([table[u] for u in units]), tokens, cotangent, *after)


def combine(outputs, after=()):
    width = 512
    arrays = []
    for pieces in outputs:
        for size, terms in pieces:
            for array, _ in terms:
                if not any(array is known for known in arrays):
                    arrays.append(array)
    width = arrays[0].shape[1]
    index = lambda array: next(i for i, known in enumerate(arrays) if known is array)
    plan = [[(size, [(index(array), start) for array, start in terms]) for size, terms in pieces] for pieces in outputs]
    shapes = [(sum(size for size, _ in pieces), width) for pieces in outputs]

    def kernel(*refs):
        in_refs, out_refs = refs[: len(arrays)], refs[len(arrays) + len(after) :]
        for pieces, out_ref in zip(plan, out_refs):
            at = 0
            for size, terms in pieces:
                total = None
                for i, start in terms:
                    value = in_refs[i][start : start + size, :]
                    total = value if total is None else total + value
                out_ref[at : at + size, :] = total
                at += size

    return pl.pallas_call(
        kernel,
        out_shape=[jax.ShapeDtypeStruct(s, F32) for s in shapes],
        in_specs=[VMEM] * len(arrays) + [ANY] * len(after),
        out_specs=[VMEM] * len(shapes),
        compiler_params=pltpu.CompilerParams(vmem_limit_bytes=16 << 20),
        cost_estimate=COST,
    )(*arrays, *after)


def sort_index(kept_index, place, blocks_in_row, after=()):
    replicas, keep, blocks = kept_index.shape
    rows = blocks // blocks_in_row
    group = replicas // 2
    lanes = PART * blocks_in_row
    segments = blocks // lanes

    def kernel(place_ref, own_ref, group_ref, *refs):
        own_out, group_out = refs[len(after) :]
        taken = place_ref[3]
        lane = lax.broadcasted_iota(jnp.int32, (lanes, PART), 0)
        row = lax.broadcasted_iota(jnp.int32, (lanes, PART), 1)
        offset = lane - row * blocks_in_row
        own = jnp.concatenate([own_ref[0, :, s * lanes : (s + 1) * lanes] for s in range(segments)], axis=0)
        own = own.astype(F32).astype(BF16)
        for c in range(blocks_in_row):
            pick = jnp.where(offset == c, 1.0, 0.0).astype(BF16)
            found = jnp.dot(own, pick, preferred_element_type=F32)
            for s in range(segments):
                own_out[c, :, s * PART : (s + 1) * PART] = found[s * keep : (s + 1) * keep]
        pick = jnp.where(offset == taken, 1.0, 0.0).astype(BF16)
        for s in range(segments // 2):
            part = group_ref[:, :, s * lanes : (s + 1) * lanes].reshape(group * keep, lanes)
            found = jnp.dot(part.astype(F32).astype(BF16), pick, preferred_element_type=F32)
            group_out[:, :, s * PART : (s + 1) * PART] = found.reshape(group, keep, PART)

    return pl.pallas_call(
        kernel,
        out_shape=[
            jax.ShapeDtypeStruct((blocks_in_row, keep, rows), F32),
            jax.ShapeDtypeStruct((group, keep, rows // 2), F32),
        ],
        grid_spec=pltpu.PrefetchScalarGridSpec(
            num_scalar_prefetch=1,
            grid=(1,),
            in_specs=[
                pl.BlockSpec((1, keep, blocks), lambda i, t: (t[0], 0, 0)),
                pl.BlockSpec((group, keep, blocks // 2), lambda i, t: (t[1], 0, t[2])),
            ]
            + [ANY] * len(after),
            out_specs=[
                pl.BlockSpec((blocks_in_row, keep, rows), lambda i, t: (0, 0, 0)),
                pl.BlockSpec((group, keep, rows // 2), lambda i, t: (0, 0, 0)),
            ],
        ),
        compiler_params=pltpu.CompilerParams(vmem_limit_bytes=24 << 20),
        cost_estimate=COST,
    )(place, kept_index, kept_index, *after)


def select(parts, momentum, half, factor, chosen, forward_cos, kept):
    before = [] if kept is None else [kept]
    width = momentum.shape[1]
    pairs = width // (2 * BLOCK)

    def kernel(*refs):
        part_refs = refs[: len(parts)]
        momentum_ref, chosen_ref, cos_ref = refs[len(parts) : len(parts) + 3]
        kept_ref, moment_ref, masked_ref = refs[-3:]
        if before:
            kept_ref[2 * pairs :] = refs[len(parts) + 3][...]
        bounds = sorted({p[2] for p in parts} | {HALF})
        sums = []
        for low, high in zip(bounds[:-1], bounds[1:]):
            total = None
            for (_, start, at, size), ref in zip(parts, part_refs):
                if at <= low and at + size >= high:
                    piece = ref[start + low - at : start + high - at, :]
                    total = piece if total is None else total + piece
            sums.append(total)
        gradient = sums[0] if len(sums) == 1 else jnp.concatenate(sums, axis=0)
        moment = DECAY * momentum_ref[half * HALF : (half + 1) * HALF, :] + factor * gradient
        moment_ref[...] = moment
        high, low = halves(moment)
        frequency = lax.broadcasted_iota(jnp.int32, (BLOCK, HALF), 0).astype(F32)
        for g in range(pairs):
            columns = slice(2 * BLOCK * g, 2 * BLOCK * (g + 1))
            values = jnp.concatenate([high[:, columns], low[:, columns], high[:, columns]], axis=1)
            spectrum = lax.dot_general(cos_ref[...], values, (((1,), (1,)), ((), ())), preferred_element_type=F32)
            for s in range(2):
                own = spectrum[s * BLOCK : (s + 1) * BLOCK]
                c = 2 * g + s
                filled = jnp.zeros_like(own)
                for j in range(KEEP):
                    hit = frequency == chosen_ref[c, j : j + 1, half * HALF : (half + 1) * HALF]
                    taken = jnp.where(hit, own, 0.0)
                    kept_ref[c, j : j + 1, :] = jnp.sum(taken, axis=0, keepdims=True)
                    filled = filled + taken
                masked_ref[c * BLOCK : (c + 1) * BLOCK, :] = filled

    return pl.pallas_call(
        kernel,
        out_shape=[
            jax.ShapeDtypeStruct((2 * pairs * (1 + len(before)), KEEP, HALF), F32),
            jax.ShapeDtypeStruct((HALF, width), F32),
            jax.ShapeDtypeStruct((width, HALF), F32),
        ],
        in_specs=[VMEM] * (len(parts) + 3 + len(before)),
        out_specs=[VMEM] * 3,
        compiler_params=pltpu.CompilerParams(vmem_limit_bytes=24 << 20),
        cost_estimate=COST,
    )(*[p[0] for p in parts], momentum, chosen, forward_cos, *before)


def inverse_of(spectra, inverse_cos):
    high, low = halves(spectra)
    return lax.dot_general(
        jnp.concatenate([high, low, high], axis=0), inverse_cos, (((0,), (0,)), ((), ())), preferred_element_type=F32
    )


def remain(moments, masked, inverse_cos, after=()):
    width = moments[0].shape[1]

    def kernel(*refs):
        cos = refs[4][...]
        out_ref = refs[-1]
        for half in range(2):
            for g in range(width // PART):
                columns = slice(PART * g, PART * (g + 1))
                rebuilt = inverse_of(refs[2 + half][columns, :], cos)
                out_ref[half * HALF : (half + 1) * HALF, columns] = refs[half][:, columns] - rebuilt

    return pl.pallas_call(
        kernel,
        out_shape=jax.ShapeDtypeStruct((2 * HALF, width), F32),
        in_specs=[VMEM] * 5 + [ANY] * len(after),
        out_specs=VMEM,
        compiler_params=pltpu.CompilerParams(vmem_limit_bytes=24 << 20),
        cost_estimate=COST,
    )(*moments, *masked, inverse_cos, *after)


def spread(values, chosen, after=()):
    members, keep, rows = values.shape

    def kernel(value_ref, chosen_ref, *refs):
        out_ref = refs[-1]
        frequency = lax.broadcasted_iota(jnp.int32, (BLOCK, PART), 0).astype(F32)
        for p in range(rows // PART):
            lanes = slice(p * PART, (p + 1) * PART)

            def add(m, total):
                own = jnp.zeros((BLOCK, PART), F32)
                for j in range(keep):
                    hit = frequency == chosen_ref[m, j : j + 1, lanes]
                    own = jnp.where(hit, value_ref[m, j : j + 1, lanes], own)
                return total + own

            out_ref[:, lanes] = lax.fori_loop(0, members, add, jnp.zeros((BLOCK, PART), F32), unroll=4)

    return pl.pallas_call(
        kernel,
        out_shape=jax.ShapeDtypeStruct((BLOCK, rows), F32),
        in_specs=[VMEM] * 2 + [ANY] * len(after),
        out_specs=VMEM,
        compiler_params=pltpu.CompilerParams(vmem_limit_bytes=24 << 20),
        cost_estimate=COST,
    )(values, chosen, *after)


def double(mine, swapped, copies, after=()):
    def kernel(mine_ref, swapped_ref, *refs):
        total = mine_ref[...] + swapped_ref[...]
        for i in range(copies):
            refs[-1][i] = total

    return pl.pallas_call(
        kernel,
        out_shape=jax.ShapeDtypeStruct((copies, *mine.shape), F32),
        in_specs=[VMEM] * 2 + [ANY] * len(after),
        out_specs=VMEM,
        compiler_params=pltpu.CompilerParams(vmem_limit_bytes=16 << 20),
        cost_estimate=COST,
    )(mine, swapped, *after)


def finish(mine, other, core, inverse_cos, scale):
    width, rows = mine.shape[0] * BLOCK, mine.shape[2]

    def kernel(core_ref, mine_ref, other_ref, cos_ref, out_ref):
        cos = cos_ref[...]
        for ref, half in ((mine_ref, core_ref[0]), (other_ref, 1 - core_ref[0])):
            first = pl.multiple_of(half * rows, rows)
            for g in range(width // PART):
                spectra = jnp.concatenate([ref[2 * g], ref[2 * g + 1]], axis=0)
                out_ref[pl.ds(first, rows), PART * g : PART * (g + 1)] = scale * inverse_of(spectra, cos)

    return pl.pallas_call(
        kernel,
        out_shape=jax.ShapeDtypeStruct((2 * rows, width), F32),
        in_specs=[SMEM, VMEM, VMEM, VMEM],
        out_specs=VMEM,
        compiler_params=pltpu.CompilerParams(vmem_limit_bytes=24 << 20),
        cost_estimate=COST,
    )(core, mine, other, inverse_cos)


def on_device(tokens, cotangent, momentum, kept_index):
    nx, ny = 2, 4
    nh, nz, nc = 2, 8, 2
    width = cotangent.shape[1]
    blocks_in_row = width // BLOCK
    group_size = lax.axis_size("fsdp")
    replicas = lax.axis_size("replica")
    factor = 1.0 / math.sqrt(tokens.shape[0] * group_size)
    forward_cos, inverse_cos = (jnp.asarray(m) for m in stacked_cosines())

    f = lax.axis_index("fsdp")
    x, y = f // ny, f % ny
    r = lax.axis_index("replica")
    h, z, c = r // (nz * nc), r // nc % nz, r % nc

    up = [(i, i // ny * ny + (i + 1) % ny) for i in range(nx * ny)]
    down = [(i, i // ny * ny + (i - 1) % ny) for i in range(nx * ny)]
    across = [(i, (i + ny) % (nx * ny)) for i in range(nx * ny)]
    to_up = lambda v: lax.ppermute(v, "fsdp", up)
    to_down = lambda v: lax.ppermute(v, "fsdp", down)
    to_across = lambda v: lax.ppermute(v, "fsdp", across)

    table = {
        (dx, dy, k): ((x + dx) % nx * ny + (y + dy) % ny) * 2 + k
        for dx in range(nx)
        for dy in range(ny)
        for k in range(2)
    }
    make = functools.partial(products, tokens, cotangent, table)

    far0, far1, x21 = make(
        [(0, 2, 0), (1, 2, 0), (1, 2, 1), (1, 1, 1), (1, 3, 1)], [1, 1, 3], limit=60 << 20
    )
    a1, b1, rx21 = to_up(far0), to_down(far1), to_across(x21)
    near1, near0 = make([(1, 1, 0), (0, 3, 0)], [1, 1], limit=54 << 20, after=[far0])
    a2, b2 = to_up(near1), to_down(near0)
    last0, last1, other, own, q2, q1, q3, q0, x0 = make(
        [(0, 1, 0), (1, 3, 0), (1, 0, 0), (0, 0, 0), (0, 2, 1), (0, 1, 1), (0, 3, 1), (0, 0, 1), (1, 0, 1)],
        [1] * 9,
        limit=48 << 20,
        after=[near1],
    )
    own_chosen, group_chosen = sort_index(
        kept_index, jnp.stack([r, h, c, z]).astype(jnp.int32), blocks_in_row, after=[last0]
    )
    last0, last1 = combine([[(HALF, [(last0, 0), (a1, 0)])], [(HALF, [(last1, 0), (b1, 0)])]], after=[own_chosen])
    a3, b3 = to_up(last0), to_down(last1)
    other, own, x0 = combine(
        [[(HALF, [(other, 0), (a2, 0)])], [(HALF, [(own, 0), (b2, 0)])], [(HALF, [(x0, 0)])]], after=[last0]
    )
    rx0 = to_across(x0)
    q2a, q2b = combine(
        [[(PART, [(q2, 0), (rx21, 0)])], [(PART, [(q2, PART), (rx21, PART)])]], after=[other]
    )
    qa1, qb1 = to_up(q2a), to_down(q2b)
    other, own = combine([[(HALF, [(other, 0), (b3, 0)])], [(HALF, [(own, 0), (a3, 0)])]], after=[q2a])
    received = to_across(other)
    q1, q3 = combine(
        [
            [(PART, [(q1, 0), (rx21, HALF), (qa1, 0)]), (PART, [(q1, PART), (rx21, HALF + PART)])],
            [(PART, [(q3, 0), (rx21, 2 * HALF)]), (PART, [(q3, PART), (rx21, 2 * HALF + PART), (qb1, 0)])],
        ],
        after=[other],
    )
    qa, qb = to_up(q1), to_down(q3)

    pieces1 = [(piece, 0, 0, HALF) for piece in (q0, rx0, qa, qb)]
    pieces0 = [(piece, 0, 0, HALF) for piece in (own, received)]
    kept, moment1, masked1 = select(pieces1, momentum[0], 1, factor, own_chosen, forward_cos, None)
    kept, moment0, masked0 = select(pieces0, momentum[0], 0, factor, own_chosen, forward_cos, kept)

    groups = [[i * nz * nc + j * nc + k for k in range(nc) for j in range(nz)] for i in range(nh)]
    kept = lax.all_to_all(kept, "replica", 0, 0, tiled=True, axis_index_groups=groups)
    members = group_chosen.reshape(nz, nc, KEEP, HALF).transpose(1, 0, 2, 3).reshape(nc * nz, KEEP, HALF)
    dense = spread(kept, members)
    swapped = lax.ppermute(dense, "replica", [(i, (i + nz * nc) % replicas) for i in range(replicas)])
    rest = remain([moment0, moment1], [masked0, masked1], inverse_cos, after=[dense])
    dense = double(dense, swapped, nz, after=[rest])
    along = [[i * nz * nc + j * nc + k for j in range(nz)] for i in range(nh) for k in range(nc)]
    mine = lax.all_to_all(
        dense, "replica", 0, 0, tiled=True, axis_index_groups=along
    )
    theirs = lax.ppermute(mine, "replica", [(i, i ^ 1) for i in range(replicas)])
    update = finish(mine, theirs, c.reshape(1).astype(jnp.int32), inverse_cos, 1.0 / replicas)
    return rest[None], update


def solution(mesh):
    in_specs = (
        P(("replica", "fsdp"), None),
        P(("replica", "fsdp"), None),
        P("replica", "fsdp", None),
        P(None, None, "fsdp"),
    )
    out_specs = (P("replica", "fsdp", None), P("fsdp", None))
    return jax.shard_map(
        on_device, mesh=mesh, in_specs=in_specs, out_specs=out_specs, check_vma=False
    )
```

time: 490 us -> 123 us (0.25)
  waiting for transfers between devices: 172 us -> 28.6 us
  local copies, waits for them, and re-layouts: 145 us -> 10.9 us
  other arithmetic: 72.5 us -> 0.71 us
  loops' own time: 62.4 us -> 0 us
  starting transfers between devices: 0.08 us -> 38.7 us
  Pallas kernels: 0 us -> 24.5 us
  matrix products: 20.7 us -> 0 us
  blocking collectives: 0 us -> 17.9 us
  between operations: 14.2 us -> 0.96 us
    slice x66 -> x0, local copies, waits for them, and re-layouts: 112 us -> none  [the longest x34 57.9 us: densify(): chosen[member_slot][None, :]]
    reduce_scatter x1 -> x0, waiting for transfers between devices: 96.1 us -> none  [on_device(): lax.psum_scatter(lax.dot_general(tokens, cotangent, (((0,), (0,)), ((), (...]
    all_gather x1 -> x0, waiting for transfers between devices: 75.8 us -> none  [on_device(): piece = lax.all_gather(kept_values[None], 'replica', axis=0, tiled=True)]
    another operation x1 -> x0, loops' own time: 62.4 us -> none  [on_device(): filled_all = lax.map(spread_one, (piece, positions))]
    dynamic_update_slice x32 -> x0, other arithmetic: 57.2 us -> none  [on_device(): filled_all = lax.map(spread_one, (piece, positions))]
    ppermute x0 -> x15, starting transfers between devices: none -> 25.5 us  [the longest x5 14.9 us: on_device(): to_down = lambda v: lax.ppermute(v, 'fsdp', down)]
    pallas_call x0 -> x15, Pallas kernels: none -> 24.5 us  [the longest x3 14 us: products(): pl.pallas_call(kernel, out_shape=[jax.ShapeDtypeStruct(s, F32) for s in s...]
    ppermute x0 -> x15, waiting for transfers between devices: none -> 21.3 us  [the longest x5 14.3 us: on_device(): to_up = lambda v: lax.ppermute(v, 'fsdp', up)]
  transfers between devices with their start and end apart: 2 -> 16, of which waited for: 2 -> 9; matrix products, arithmetic and copies ran while one was open for 3% -> 1% of each run, Pallas kernels for 0% -> 13%
where the time goes in v1:
time: 123 us; the launch traced here: 122 us
  starting transfers between devices  38.7 us (31%)
  waiting for transfers between devices  28.6 us (23%)
  Pallas kernels  24.5 us (20%)
  blocking collectives  17.9 us (15%)
  local copies, waits for them, and re-layouts  10.9 us (9%)
    all_to_all x1, blocking collectives, on_device(): lax.all_to_all(dense, 'replica', 0, 0, tiled=True, axis_index_groups=along)  17.9 us
    ppermute x5, starting transfers between devices, on_device(): to_down = lambda v: lax.ppermute(v, 'fsdp', down)  14.9 us
    ppermute x5, waiting for transfers between devices, on_device(): to_up = lambda v: lax.ppermute(v, 'fsdp', up)  14.3 us
    pallas_call x3, Pallas kernels, products(): pl.pallas_call(kernel, out_shape=[jax.ShapeDtypeStruct(s, F32) for s in s...  14 us
    all_to_all x1, starting transfers between devices, on_device(): lax.all_to_all(kept, 'replica', 0, 0, tiled=True, axis_index_groups=groups)  13.2 us
    unnamed x42, local copies, waits for them, and re-layouts  10.2 us
    all_to_all x1, waiting for transfers between devices, on_device(): lax.all_to_all(kept, 'replica', 0, 0, tiled=True, axis_index_groups=groups)  7.28 us
    ppermute x3, starting transfers between devices, on_device(): to_across = lambda v: lax.ppermute(v, 'fsdp', across)  3.99 us
  transfers between devices with their start and end apart: 16, of which 9 were waited for; matrix products, arithmetic and copies ran while one was open for 1% of the time, Pallas kernels for 13%

profile of v1, /device:TPU:1, one launch (start us, length us, event | category | flops | bytes accessed | tf_op | source)
XLA Modules:
  0.0 122.3 jit_solution(2872459479166456946)
XLA Ops:
  1.3 5.2 %shard_map.77 = (f32[256,512]{1,0:T(8,128)}, f32[256,512]{1,0:T(8,128)}, f32[768,512]{1,0:T(8,128)}) custom-call(s32[5]{0:T(128)} %stack.90.table_ref, bf16[640,4096]{1,0:T(8,128)(2,1)} %tokens_ref.5, bf16[640,512]{1,0:T(8,128)(2,1)} %cot_ref.5), custom_call_target="tpu_custom_call" | custom-call | flops 1 | bytes 1 | tf_op jit(solution)/shard_map/pallas_call | solution.py:81
  6.6 2.1 %collective-permute-start.6 = (f32[768,512]{1,0:T(8,128)}, f32[768,512]{1,0:T(8,128)S(1)}, u32[]{:S(2)}, u32[]{:S(2)}) collective-permute-start(f32[768,512]{1,0:T(8,128)} %get-tuple-element.50), channel_id=1, source_target_pairs={{0,4},{1,5},{2,6},{3,7},{4,0},{5,1},{6,2},{7,3},{8,12},{9,13},{10,... | collective-permute-start | bytes 4718600 | tf_op jit(solution)/shard_map/ppermute | solution.py:345
  8.7 2.7 %collective-permute-start.3 = (f32[256,512]{1,0:T(8,128)}, f32[256,512]{1,0:T(8,128)}, u32[]{:S(2)}, u32[]{:S(2)}) collective-permute-start(f32[256,512]{1,0:T(8,128)} %get-tuple-element.43), channel_id=1, source_target_pairs={{0,3},{1,0},{2,1},{3,2},{4,7},{5,4},{6,5},{7,6},{8,11},{9,8},{10,9... | collective-permute-start | bytes 1572872 | tf_op jit(solution)/shard_map/ppermute | solution.py:344
  12.1 3.7 %shard_map.78 = (f32[256,512]{1,0:T(8,128)}, f32[256,512]{1,0:T(8,128)}) custom-call(s32[2]{0:T(128)} %pad_add_fusion.table_ref, bf16[640,4096]{1,0:T(8,128)(2,1)} %tokens_ref.5, bf16[640,512]{1,0:T(8,128)(2,1)} %cot_ref.5, f32[256,512]{1,0:T(8,128)} %get-tuple-element.35.refs_0_), custom_call_target="tpu_custom_call" | custom-call | flops 1 | bytes 1 | tf_op jit(solution)/shard_map/pallas_call | solution.py:81
  15.8 2.8 %collective-permute-start.1 = (f32[256,512]{1,0:T(8,128)}, f32[256,512]{1,0:T(8,128)}, u32[]{:S(2)}, u32[]{:S(2)}) collective-permute-start(f32[256,512]{1,0:T(8,128)} %get-tuple-element.39), channel_id=1, source_target_pairs={{0,3},{1,0},{2,1},{3,2},{4,7},{5,4},{6,5},{7,6},{8,11},{9,8},{10,9... | collective-permute-start | bytes 1572872 | tf_op jit(solution)/shard_map/ppermute | solution.py:344
  18.6 1.0 copy-done.4
  19.7 5.1 %shard_map.79 = (f32[256,512]{1,0:T(8,128)S(1)}, f32[256,512]{1,0:T(8,128)S(1)}, f32[256,512]{1,0:T(8,128)S(1)}, f32[256,512]{1,0:T(8,128)S(1)}, f32[256,512]{1,...) custom-call(s32[9]{0:T(128)S(1)} %stack.81.table_ref, ...), custom_call_target="tpu_custom_call" | custom-call | flops 1 | bytes 1 | tf_op jit(solution)/shard_map/pallas_call | solution.py:81
  29.7 0.8 copy-done.17
  30.6 2.2 %copy-done = s32[32,8,4096]{2,1,0:T(8,128)S(1)} copy-done((s32[32,8,4096]{2,1,0:T(8,128)S(1)}, s32[32,8,4096]{2,1,0:T(8,128)}, u32[]{:S(2)}) %copy-start) | copy-done | bytes 4194328
  32.8 1.2 shard_map.80
  34.0 1.4 %shard_map.81 = (f32[256,512]{1,0:T(8,128)S(1)}, f32[256,512]{1,0:T(8,128)S(1)}) custom-call(f32[256,512]{1,0:T(8,128)S(1)} %get-tuple-element.41.refs_0_, f32[256,512]{1,0:T(8,128)} %collective-permute-done.2.refs_1_, f32[256,512]{1,0:T(8,128)S(1)} %copy-done.12, f32[256,512]{1,0:T(8,128)} %collective-permute-done.3.refs_3_, ...), custom_call_target="tpu_custom_call" | custom-call | flops 1 | bytes 1 | tf_op jit(solution)/shard_map/pallas_call | solution.py:117
  35.4 2.8 %collective-permute-start.4 = (f32[256,512]{1,0:T(8,128)S(1)}, f32[256,512]{1,0:T(8,128)S(1)}, u32[]{:S(2)}, u32[]{:S(2)}) collective-permute-start(f32[256,512]{1,0:T(8,128)S(1)} %get-tuple-element.47), channel_id=1, source_target_pairs={{0,3},{1,0},{2,1},{3,2},{4,7},{5,4},{6,5},{7,6},{8,11},{9,8},{10,9... | collective-permute-start | bytes 1572872 | tf_op jit(solution)/shard_map/ppermute | solution.py:344
  38.2 1.3 %shard_map.82 = (f32[256,512]{1,0:T(8,128)S(1)}, f32[256,512]{1,0:T(8,128)S(1)}, f32[256,512]{1,0:T(8,128)S(1)}) custom-call(f32[256,512]{1,0:T(8,128)S(1)} %copy-done.14, f32[256,512]{1,0:T(8,128)} %collective-permute-done.refs_1_, f32[256,512]{1,0:T(8,128)S(1)} %copy-done.16, f32[256,512]{1,0:T(8,128)} %collective-permute-done.1.refs_3_, ...), custom_call_target="tpu_custom_call" | custom-call | flops 1 | bytes 1 | tf_op jit(solution)/shard_map/pallas_call | solution.py:117
  39.5 2.3 %collective-permute-done.6.refs_1_ = f32[768,512]{1,0:T(8,128)S(1)} collective-permute-done((f32[768,512]{1,0:T(8,128)}, f32[768,512]{1,0:T(8,128)S(1)}, u32[]{:S(2)}, u32[]{:S(2)}) %collective-permute-start.6) | collective-permute-done | bytes 1572896 | tf_op jit(solution)/shard_map/ppermute | solution.py:345
  41.9 4.0 %collective-permute-start.10 = (f32[128,512]{1,0:T(8,128)S(1)}, f32[128,512]{1,0:T(8,128)S(1)}, u32[]{:S(2)}, u32[]{:S(2)}) collective-permute-start(f32[128,512]{1,0:T(8,128)S(1)} %get-tuple-element.58), channel_id=1, source_target_pairs={{0,3},{1,0},{2,1},{3,2},{4,7},{5,4},{6,5},{7,6},{8,11},{9,8},{10,9... | collective-permute-start | bytes 786440 | tf_op jit(solution)/shard_map/ppermute | solution.py:344
  45.9 1.2 collective-permute-start.8
  47.3 3.1 %collective-permute-done.5.refs_3_ = f32[256,512]{1,0:T(8,128)S(1)} collective-permute-done((f32[256,512]{1,0:T(8,128)S(1)}, f32[256,512]{1,0:T(8,128)S(1)}, u32[]{:S(2)}, u32[]{:S(2)}) %collective-permute-start.5) | collective-permute-done | bytes 524320 | tf_op jit(solution)/shard_map/ppermute | solution.py:343
  50.5 2.4 %collective-permute-done.10.refs_4_ = f32[128,512]{1,0:T(8,128)S(1)} collective-permute-done((f32[128,512]{1,0:T(8,128)S(1)}, f32[128,512]{1,0:T(8,128)S(1)}, u32[]{:S(2)}, u32[]{:S(2)}) %collective-permute-start.10) | collective-permute-done | bytes 262176 | tf_op jit(solution)/shard_map/ppermute | solution.py:344
  52.9 3.1 %collective-permute-done.9.refs_2_ = f32[128,512]{1,0:T(8,128)S(1)} collective-permute-done((f32[128,512]{1,0:T(8,128)S(1)}, f32[128,512]{1,0:T(8,128)S(1)}, u32[]{:S(2)}, u32[]{:S(2)}) %collective-permute-start.9) | collective-permute-done | bytes 262176 | tf_op jit(solution)/shard_map/ppermute | solution.py:343
  56.5 2.7 %collective-permute-start.12 = (f32[256,512]{1,0:T(8,128)S(1)}, f32[256,512]{1,0:T(8,128)S(1)}, u32[]{:S(2)}, u32[]{:S(2)}) collective-permute-start(f32[256,512]{1,0:T(8,128)S(1)} %get-tuple-element.60), channel_id=1, source_target_pairs={{0,3},{1,0},{2,1},{3,2},{4,7},{5,4},{6,5},{7,6},{8,11},{9,8},{10,9... | collective-permute-start | bytes 1572872 | tf_op jit(solution)/shard_map/ppermute | solution.py:344
  59.8 8.0 %collective-permute-done.11.refs_2_ = f32[256,512]{1,0:T(8,128)S(1)} collective-permute-done((f32[256,512]{1,0:T(8,128)S(1)}, f32[256,512]{1,0:T(8,128)S(1)}, u32[]{:S(2)}, u32[]{:S(2)}) %collective-permute-start.11) | collective-permute-done | bytes 524320 | tf_op jit(solution)/shard_map/ppermute | solution.py:343
  67.8 0.9 shard_map.86
  68.8 1.6 %shard_map.87 = (f32[16,8,256]{2,1,0:T(8,128)}, f32[256,512]{1,0:T(8,128)S(1)}, f32[512,256]{1,0:T(8,128)S(1)}) custom-call(f32[256,512]{1,0:T(8,128)S(1)} %get-tuple-element.52.refs_0_, f32[256,512]{1,0:T(8,128)S(1)} %collective-permute-done.7.refs_1_, f32[512,512]{1,0:T(8,128)S(1)} %bitcast.27, f32[8,8,512]{2,1,0:T(8,128)S(1)} %get-tuple-element.44.refs_4_.refs_5_.refs_3_, ...), custom_call_target="tpu_custom_call" | custom-call | flops 1 | bytes 1 | tf_op jit(solution)/shard_map/pallas_call | solution.py:217
  70.3 13.2 %all-to-all-start = ((f32[16,8,256]{2,1,0:T(8,128)}), f32[16,8,256]{2,1,0:T(8,128)S(1)}, u32[]{:S(2)}, u32[]{:S(2)}) async-start(f32[16,8,256]{2,1,0:T(8,128)} %get-tuple-element.66), calls=%async_computation | async-start | bytes 262144 | tf_op jit(solution)/shard_map/all_to_all | solution.py:397
  83.5 7.3 %all-to-all-done.value_ref = f32[16,8,256]{2,1,0:T(8,128)S(1)} async-done(((f32[16,8,256]{2,1,0:T(8,128)}), f32[16,8,256]{2,1,0:T(8,128)S(1)}, u32[]{:S(2)}, u32[]{:S(2)}) %all-to-all-start) | async-done | bytes 131104 | tf_op jit(solution)/shard_map/all_to_all | solution.py:397
  91.4 2.5 %collective-permute-start.13 = (f32[64,256]{1,0:T(8,128)S(1)}, f32[64,256]{1,0:T(8,128)S(1)}, u32[]{:S(2)}, u32[]{:S(2)}) collective-permute-start(f32[64,256]{1,0:T(8,128)S(1)} %shard_map.88.refs_5_.mine_ref), channel_id=1, source_target_pairs={{0,128},{8,136},{16,144},{24,152},{32,160},{40,168},{48,176},{56,1... | collective-permute-start | bytes 196616 | tf_op jit(solution)/shard_map/ppermute | solution.py:400
  94.0 1.6 %shard_map.89.refs_0_ = f32[512,512]{1,0:T(8,128)} custom-call(f32[256,512]{1,0:T(8,128)S(1)} %get-tuple-element.62.refs_0_, f32[256,512]{1,0:T(8,128)S(1)} %get-tuple-element.63.refs_1_, f32[512,256]{1,0:T(8,128)S(1)} %get-tuple-element.64.refs_2_, f32[512,256]{1,0:T(8,128)S(1)} %get-tuple-element.65.refs_3_, bf16[384,128]{1,0:T(8,128)(2,1)S(1)} %copy-done.19, ...), custom_call_target="tpu_custom_call" | custom-call | flops 1 | bytes 1 | tf_op jit(solution)/shard_map/pallas_call | solution.py:250
  96.1 1.2 %copy-done.3 = f32[512,512]{1,0:T(8,128)S(1)} copy-done((f32[512,512]{1,0:T(8,128)S(1)}, f32[512,512]{1,0:T(8,128)}, u32[]{:S(2)}) %copy-start.3) | copy-done | bytes 1048600
  97.4 17.9 %all_to_all.10.mine_ref = f32[8,64,256]{2,1,0:T(8,128)S(1)} all-to-all(f32[8,64,256]{2,1,0:T(8,128)S(1)} %shard_map.90), channel_id=1, replica_groups={{0,16,32,48,64,80,96,112},{8,24,40,56,72,88,104,120},{128,144,160,176,1..., dimensions={0} | all-to-all | bytes 1048576 | tf_op jit(solution)/shard_map/all_to_all | solution.py:404
  115.3 3.9 %collective-permute-start.14 = (f32[8,64,256]{2,1,0:T(8,128)S(1)}, f32[8,64,256]{2,1,0:T(8,128)S(1)}, u32[]{:S(2)}, u32[]{:S(2)}) collective-permute-start(f32[8,64,256]{2,1,0:T(8,128)S(1)} %all_to_all.10.mine_ref), channel_id=1, source_target_pairs={{0,8},{8,0},{16,24},{24,16},{32,40},{40,32},{48,56},{56,48},{64,72... | collective-permute-start | bytes 1572872 | tf_op jit(solution)/shard_map/ppermute | solution.py:407
  119.2 1.5 %collective-permute-done.14.other_ref = f32[8,64,256]{2,1,0:T(8,128)S(1)} collective-permute-done((f32[8,64,256]{2,1,0:T(8,128)S(1)}, f32[8,64,256]{2,1,0:T(8,128)S(1)}, u32[]{:S(2)}, u32[]{:S(2)}) %collective-permute-start.14) | collective-permute-done | bytes 524320 | tf_op jit(solution)/shard_map/ppermute | solution.py:407
  120.7 1.6 %shard_map.91 = f32[512,512]{1,0:T(8,128)} custom-call(s32[1]{0:T(128)} %bitcast.18.core_ref, f32[8,64,256]{2,1,0:T(8,128)S(1)} %all_to_all.10.mine_ref, f32[8,64,256]{2,1,0:T(8,128)S(1)} %collective-permute-done.14.other_ref, bf16[384,128]{1,0:T(8,128)(2,1)S(1)} %copy-done.19), custom_call_target="tpu_custom_call" | custom-call | flops 1 | bytes 1 | tf_op jit(solution)/shard_map/pallas_call | solution.py:315
  (63 shorter events, 9.0 us)
Async XLA Ops:
  6.6 12.0 %copy-start.1 = (bf16[640,512]{1,0:T(8,128)(2,1)S(1)}, bf16[640,512]{1,0:T(8,128)(2,1)}, u32[]{:S(2)}) copy-start(bf16[640,512]{1,0:T(8,128)(2,1)} %cot_ref.5) | copy-start | bytes 1966084
  6.6 35.2 %collective-permute-start.6 = (f32[768,512]{1,0:T(8,128)}, f32[768,512]{1,0:T(8,128)S(1)}, u32[]{:S(2)}, u32[]{:S(2)}) collective-permute-start(f32[768,512]{1,0:T(8,128)} %get-tuple-element.50), channel_id=1, source_target_pairs={{0,4},{1,5},{2,6},{3,7},{4,0},{5,1},{6,2},{7,3},{8,12},{9,13},{10,... | collective-permute-start | bytes 4718600 | tf_op jit(solution)/shard_map/ppermute | solution.py:345
  8.7 25.3 %collective-permute-start.3 = (f32[256,512]{1,0:T(8,128)}, f32[256,512]{1,0:T(8,128)}, u32[]{:S(2)}, u32[]{:S(2)}) collective-permute-start(f32[256,512]{1,0:T(8,128)} %get-tuple-element.43), channel_id=1, source_target_pairs={{0,3},{1,0},{2,1},{3,2},{4,7},{5,4},{6,5},{7,6},{8,11},{9,8},{10,9... | collective-permute-start | bytes 1572872 | tf_op jit(solution)/shard_map/ppermute | solution.py:344
  11.5 22.5 %collective-permute-start.2 = (f32[256,512]{1,0:T(8,128)}, f32[256,512]{1,0:T(8,128)}, u32[]{:S(2)}, u32[]{:S(2)}) collective-permute-start(f32[256,512]{1,0:T(8,128)} %get-tuple-element.35.refs_0_), channel_id=1, source_target_pairs={{0,1},{1,2},{2,3},{3,0},{4,5},{5,6},{6,7},{7,4},{8,9},{9,10},{10,1... | collective-permute-start | bytes 1572872 | tf_op jit(solution)/shard_map/ppermute | solution.py:343
  15.8 22.4 %collective-permute-start.1 = (f32[256,512]{1,0:T(8,128)}, f32[256,512]{1,0:T(8,128)}, u32[]{:S(2)}, u32[]{:S(2)}) collective-permute-start(f32[256,512]{1,0:T(8,128)} %get-tuple-element.39), channel_id=1, source_target_pairs={{0,3},{1,0},{2,1},{3,2},{4,7},{5,4},{6,5},{7,6},{8,11},{9,8},{10,9... | collective-permute-start | bytes 1572872 | tf_op jit(solution)/shard_map/ppermute | solution.py:344
  18.5 19.6 %collective-permute-start = (f32[256,512]{1,0:T(8,128)}, f32[256,512]{1,0:T(8,128)}, u32[]{:S(2)}, u32[]{:S(2)}) collective-permute-start(f32[256,512]{1,0:T(8,128)} %get-tuple-element.36.refs_0_), channel_id=1, source_target_pairs={{0,1},{1,2},{2,3},{3,0},{4,5},{5,6},{6,7},{7,4},{8,9},{9,10},{10,1... | collective-permute-start | bytes 1572872 | tf_op jit(solution)/shard_map/ppermute | solution.py:343
  18.6 1.0 copy-start.4
  24.8 0.8 copy-start.5
  29.7 0.9 copy-start.17
  30.6 2.2 %copy-start = (s32[32,8,4096]{2,1,0:T(8,128)S(1)}, s32[32,8,4096]{2,1,0:T(8,128)}, u32[]{:S(2)}) copy-start(s32[32,8,4096]{2,1,0:T(8,128)} %group_ref.1) | copy-start | bytes 12582916
  32.8 1.2 copy-start.12
  32.8 5.4 %copy-start.14 = (f32[256,512]{1,0:T(8,128)S(1)}, f32[256,512]{1,0:T(8,128)}, u32[]{:S(2)}) copy-start(f32[256,512]{1,0:T(8,128)} %copy-done.13) | copy-start | bytes 1572868
  32.8 5.4 %copy-start.16 = (f32[256,512]{1,0:T(8,128)S(1)}, f32[256,512]{1,0:T(8,128)}, u32[]{:S(2)}) copy-start(f32[256,512]{1,0:T(8,128)} %copy-done.15) | copy-start | bytes 1572868
  32.8 5.4 %copy-start.18 = (f32[256,512]{1,0:T(8,128)S(1)}, f32[256,512]{1,0:T(8,128)}, u32[]{:S(2)}) copy-start(f32[256,512]{1,0:T(8,128)} %copy-done.17) | copy-start | bytes 1572868
  34.0 7.9 %copy-start.10 = (f32[256,512]{1,0:T(8,128)S(1)}, f32[256,512]{1,0:T(8,128)}, u32[]{:S(2)}) copy-start(f32[256,512]{1,0:T(8,128)} %copy-done.9) | copy-start | bytes 1572868
  35.4 20.7 %copy-start.6 = (f32[256,512]{1,0:T(8,128)S(1)}, f32[256,512]{1,0:T(8,128)}, u32[]{:S(2)}) copy-start(f32[256,512]{1,0:T(8,128)} %copy-done.5) | copy-start | bytes 1572868
  35.4 20.7 %copy-start.8 = (f32[256,512]{1,0:T(8,128)S(1)}, f32[256,512]{1,0:T(8,128)}, u32[]{:S(2)}) copy-start(f32[256,512]{1,0:T(8,128)} %copy-done.7) | copy-start | bytes 1572868
  35.4 11.9 %collective-permute-start.4 = (f32[256,512]{1,0:T(8,128)S(1)}, f32[256,512]{1,0:T(8,128)S(1)}, u32[]{:S(2)}, u32[]{:S(2)}) collective-permute-start(f32[256,512]{1,0:T(8,128)S(1)} %get-tuple-element.47), channel_id=1, source_target_pairs={{0,3},{1,0},{2,1},{3,2},{4,7},{5,4},{6,5},{7,6},{8,11},{9,8},{10,9... | collective-permute-start | bytes 1572872 | tf_op jit(solution)/shard_map/ppermute | solution.py:344
  38.2 12.3 %collective-permute-start.5 = (f32[256,512]{1,0:T(8,128)S(1)}, f32[256,512]{1,0:T(8,128)S(1)}, u32[]{:S(2)}, u32[]{:S(2)}) collective-permute-start(f32[256,512]{1,0:T(8,128)S(1)} %get-tuple-element.45.refs_5_), channel_id=1, source_target_pairs={{0,1},{1,2},{2,3},{3,0},{4,5},{5,6},{6,7},{7,4},{8,9},{9,10},{10,1... | collective-permute-start | bytes 1572872 | tf_op jit(solution)/shard_map/ppermute | solution.py:343
  41.8 26.0 %copy-start.2 = (f32[1,512,512]{2,1,0:T(8,128)S(1)}, f32[1,512,512]{2,1,0:T(8,128)}, u32[]{:S(2)}) copy-start(f32[1,512,512]{2,1,0:T(8,128)} %param.8) | copy-start | bytes 3145732
  41.8 26.0 %copy-start.20 = (bf16[128,384]{1,0:T(8,128)(2,1)S(1)}, bf16[128,384]{1,0:T(8,128)(2,1)}, u32[]{:S(2)}) copy-start(bf16[128,384]{1,0:T(8,128)(2,1)} %constant.153.clone.refs_6_.refs_4_) | copy-start | bytes 294916
  41.9 11.0 %collective-permute-start.10 = (f32[128,512]{1,0:T(8,128)S(1)}, f32[128,512]{1,0:T(8,128)S(1)}, u32[]{:S(2)}, u32[]{:S(2)}) collective-permute-start(f32[128,512]{1,0:T(8,128)S(1)} %get-tuple-element.58), channel_id=1, source_target_pairs={{0,3},{1,0},{2,1},{3,2},{4,7},{5,4},{6,5},{7,6},{8,11},{9,8},{10,9... | collective-permute-start | bytes 786440 | tf_op jit(solution)/shard_map/ppermute | solution.py:344
  45.9 10.2 %collective-permute-start.9 = (f32[128,512]{1,0:T(8,128)S(1)}, f32[128,512]{1,0:T(8,128)S(1)}, u32[]{:S(2)}, u32[]{:S(2)}) collective-permute-start(f32[128,512]{1,0:T(8,128)S(1)} %get-tuple-element.51.refs_4_), channel_id=1, source_target_pairs={{0,1},{1,2},{2,3},{3,0},{4,5},{5,6},{6,7},{7,4},{8,9},{9,10},{10,1... | collective-permute-start | bytes 786440 | tf_op jit(solution)/shard_map/ppermute | solution.py:343
  45.9 13.9 %collective-permute-start.8 = (f32[256,512]{1,0:T(8,128)S(1)}, f32[256,512]{1,0:T(8,128)S(1)}, u32[]{:S(2)}, u32[]{:S(2)}) collective-permute-start(f32[256,512]{1,0:T(8,128)S(1)} %get-tuple-element.55), channel_id=1, source_target_pairs={{0,4},{1,5},{2,6},{3,7},{4,0},{5,1},{6,2},{7,3},{8,12},{9,13},{10,... | collective-permute-start | bytes 1572872 | tf_op jit(solution)/shard_map/ppermute | solution.py:345
  56.2 37.8 %copy-start.19 = (bf16[384,128]{1,0:T(8,128)(2,1)S(1)}, bf16[384,128]{1,0:T(8,128)(2,1)}, u32[]{:S(2)}) copy-start(bf16[384,128]{1,0:T(8,128)(2,1)} %constant.154.clone.refs_4_.cos_ref) | copy-start | bytes 294916
  56.2 11.6 %collective-permute-start.11 = (f32[256,512]{1,0:T(8,128)S(1)}, f32[256,512]{1,0:T(8,128)S(1)}, u32[]{:S(2)}, u32[]{:S(2)}) collective-permute-start(f32[256,512]{1,0:T(8,128)S(1)} %get-tuple-element.59), channel_id=1, source_target_pairs={{0,1},{1,2},{2,3},{3,0},{4,5},{5,6},{6,7},{7,4},{8,9},{9,10},{10,1... | collective-permute-start | bytes 1572872 | tf_op jit(solution)/shard_map/ppermute | solution.py:343
  56.5 11.3 %collective-permute-start.12 = (f32[256,512]{1,0:T(8,128)S(1)}, f32[256,512]{1,0:T(8,128)S(1)}, u32[]{:S(2)}, u32[]{:S(2)}) collective-permute-start(f32[256,512]{1,0:T(8,128)S(1)} %get-tuple-element.60), channel_id=1, source_target_pairs={{0,3},{1,0},{2,1},{3,2},{4,7},{5,4},{6,5},{7,6},{8,11},{9,8},{10,9... | collective-permute-start | bytes 1572872 | tf_op jit(solution)/shard_map/ppermute | solution.py:344
  59.1 9.6 %collective-permute-start.7 = (f32[256,512]{1,0:T(8,128)S(1)}, f32[256,512]{1,0:T(8,128)S(1)}, u32[]{:S(2)}, u32[]{:S(2)}) collective-permute-start(f32[256,512]{1,0:T(8,128)S(1)} %get-tuple-element.53.refs_5_), channel_id=1, source_target_pairs={{0,4},{1,5},{2,6},{3,7},{4,0},{5,1},{6,2},{7,3},{8,12},{9,13},{10,... | collective-permute-start | bytes 1572872 | tf_op jit(solution)/shard_map/ppermute | solution.py:345
  70.3 20.5 %all-to-all-start = ((f32[16,8,256]{2,1,0:T(8,128)}), f32[16,8,256]{2,1,0:T(8,128)S(1)}, u32[]{:S(2)}, u32[]{:S(2)}) async-start(f32[16,8,256]{2,1,0:T(8,128)} %get-tuple-element.66), calls=%async_computation | async-start | bytes 262144 | tf_op jit(solution)/shard_map/all_to_all | solution.py:397
  91.4 4.7 %collective-permute-start.13 = (f32[64,256]{1,0:T(8,128)S(1)}, f32[64,256]{1,0:T(8,128)S(1)}, u32[]{:S(2)}, u32[]{:S(2)}) collective-permute-start(f32[64,256]{1,0:T(8,128)S(1)} %shard_map.88.refs_5_.mine_ref), channel_id=1, source_target_pairs={{0,128},{8,136},{16,144},{24,152},{32,160},{40,168},{48,176},{56,1... | collective-permute-start | bytes 196616 | tf_op jit(solution)/shard_map/ppermute | solution.py:400
  96.1 1.2 %copy-start.3 = (f32[512,512]{1,0:T(8,128)S(1)}, f32[512,512]{1,0:T(8,128)}, u32[]{:S(2)}) copy-start(f32[512,512]{1,0:T(8,128)} %shard_map.89.refs_0_) | copy-start | bytes 3145732
  115.3 5.4 %collective-permute-start.14 = (f32[8,64,256]{2,1,0:T(8,128)S(1)}, f32[8,64,256]{2,1,0:T(8,128)S(1)}, u32[]{:S(2)}, u32[]{:S(2)}) collective-permute-start(f32[8,64,256]{2,1,0:T(8,128)S(1)} %all_to_all.10.mine_ref), channel_id=1, source_target_pairs={{0,8},{8,0},{16,24},{24,16},{32,40},{40,32},{48,56},{56,48},{64,72... | collective-permute-start | bytes 1572872 | tf_op jit(solution)/shard_map/ppermute | solution.py:407
  (5 other events, 4.0 us)

commit v2 on v1

v2 whole, which is shorter than its diff:
```python
import functools
import math

import jax
import jax.numpy as jnp
import numpy as np
from jax import lax
from jax.experimental import pallas as pl
from jax.experimental.pallas import tpu as pltpu
from jax.sharding import PartitionSpec as P

BLOCK = 64
KEEP = 8
HALF = 256
NX, NY = 2, 4
NH, NZ, NC = 2, 8, 2
PART = 128
DECAY = 0.9
BF16 = jnp.bfloat16
F32 = jnp.float32
VMEM = pl.BlockSpec(memory_space=pltpu.VMEM)
HBM = pl.BlockSpec(memory_space=pltpu.HBM)
SMEM = pl.BlockSpec(memory_space=pltpu.SMEM)
ANY = pl.BlockSpec(memory_space=pl.ANY)
COST = pl.CostEstimate(flops=1, bytes_accessed=1, transcendentals=0)


def paired_cosines():
    k = np.arange(BLOCK, dtype=np.float64)[:, None]
    n = np.arange(BLOCK, dtype=np.float64)[None, :]
    c = np.sqrt(np.where(k == 0, 1.0, 2.0) / BLOCK) * np.cos(np.pi * (2 * n + 1) * k / (2 * BLOCK))
    both = np.zeros((2 * BLOCK, 2 * BLOCK))
    both[:BLOCK, :BLOCK] = c
    both[BLOCK:, BLOCK:] = c
    return both.astype(np.float32)


def halves(value):
    high = value.astype(BF16)
    return high, (value - high.astype(F32)).astype(BF16)


def stacked_cosines():
    pair = paired_cosines()
    high = pair.astype(jnp.bfloat16)
    low = (pair - high.astype(np.float32)).astype(jnp.bfloat16)
    return np.concatenate([high, high, low], axis=1), np.concatenate([high, high, low], axis=0)


def products(tokens, cotangent, units, counts, limit, after=()):
    depth, width = cotangent.shape
    total = len(units)
    shapes = [(HALF * count, width) for count in counts]

    def kernel(tokens_ref, cot_ref, *refs):
        out_refs, (buffer, cot, sems) = refs[len(after) : -3], refs[-3:]
        f = lax.axis_index("fsdp")
        x, y = f // NY, f % NY
        copies = [pltpu.make_async_copy(cot_ref, cot, sems.at[total])]
        for m, (dx, dy, k) in enumerate(units):
            place = (x + dx) % NX * NY + (y + dy) % NY
            column = pl.multiple_of((2 * place + k) * HALF, HALF)
            copies.append(pltpu.make_async_copy(tokens_ref.at[:, pl.ds(column, HALF)], buffer.at[m], sems.at[m]))
        for copy in copies:
            copy.start()
        copies[0].wait()
        at = 0
        for count, out_ref in zip(counts, out_refs):
            for m in range(count):
                copies[1 + at].wait()
                out_ref[m * HALF : (m + 1) * HALF, :] = lax.dot_general(
                    buffer[at], cot[...], (((0,), (0,)), ((), ())), preferred_element_type=F32
                )
                at += 1

    return pl.pallas_call(
        kernel,
        out_shape=[jax.ShapeDtypeStruct(s, F32) for s in shapes],
        in_specs=[ANY, ANY] + [ANY] * len(after),
        out_specs=[VMEM] * len(shapes),
        scratch_shapes=[
            pltpu.VMEM((total, depth, HALF), BF16),
            pltpu.VMEM((depth, width), BF16),
            pltpu.SemaphoreType.DMA((total + 1,)),
        ],
        compiler_params=pltpu.CompilerParams(vmem_limit_bytes=limit),
        cost_estimate=COST,
    )(tokens, cotangent, *after)


def combine(outputs, after=()):
    arrays = []
    for pieces in outputs:
        for size, terms in pieces:
            for array, _ in terms:
                if not any(array is known for known in arrays):
                    arrays.append(array)
    width = arrays[0].shape[1]
    index = lambda array: next(i for i, known in enumerate(arrays) if known is array)
    plan = [[(size, [(index(array), start) for array, start in terms]) for size, terms in pieces] for pieces in outputs]
    shapes = [(sum(size for size, _ in pieces), width) for pieces in outputs]

    def kernel(*refs):
        in_refs, out_refs = refs[: len(arrays)], refs[len(arrays) + len(after) :]
        for pieces, out_ref in zip(plan, out_refs):
            at = 0
            for size, terms in pieces:
                total = None
                for i, start in terms:
                    value = in_refs[i][start : start + size, :]
                    total = value if total is None else total + value
                out_ref[at : at + size, :] = total
                at += size

    return pl.pallas_call(
        kernel,
        out_shape=[jax.ShapeDtypeStruct(s, F32) for s in shapes],
        in_specs=[VMEM] * len(arrays) + [ANY] * len(after),
        out_specs=[VMEM] * len(shapes),
        compiler_params=pltpu.CompilerParams(vmem_limit_bytes=16 << 20),
        cost_estimate=COST,
    )(*arrays, *after)


def sort_index(kept_index, limit, after=()):
    replicas, keep, blocks = kept_index.shape
    rows = 2 * HALF
    in_row = blocks // rows
    lanes = PART * in_row

    def kernel(index_ref, *refs):
        own_out, all_out, own_buffer, all_buffer, sems = refs[len(after) :]
        r = lax.axis_index("replica")
        h, z, c = r // (NZ * NC), r // NC % NZ, r % NC
        first = pl.multiple_of((h * NC + c) * lanes, lanes)
        copies = [
            pltpu.make_async_copy(index_ref.at[r], own_buffer, sems.at[0]),
            pltpu.make_async_copy(index_ref.at[:, :, pl.ds(first, lanes)], all_buffer, sems.at[1]),
        ]
        for copy in copies:
            copy.start()
        lane = lax.broadcasted_iota(jnp.int32, (lanes, PART), 0)
        row = lax.broadcasted_iota(jnp.int32, (lanes, PART), 1)
        offset = lane - row * in_row
        copies[0].wait()
        own = jnp.concatenate([own_buffer[:, s * lanes : (s + 1) * lanes] for s in range(rows // PART)], axis=0)
        own = own.astype(F32).astype(BF16)
        for i in range(in_row):
            pick = jnp.where(offset == i, 1.0, 0.0).astype(BF16)
            found = jnp.dot(own, pick, preferred_element_type=F32)
            for s in range(rows // PART):
                own_out[i, :, s * PART : (s + 1) * PART] = found[s * keep : (s + 1) * keep]
        copies[1].wait()
        pick = jnp.where(offset == z, 1.0, 0.0).astype(BF16)
        found = jnp.dot(
            all_buffer[...].reshape(replicas * keep, lanes).astype(F32).astype(BF16), pick, preferred_element_type=F32
        )
        all_out[...] = found.reshape(replicas, keep, PART)

    return pl.pallas_call(
        kernel,
        out_shape=[
            jax.ShapeDtypeStruct((in_row, keep, rows), F32),
            jax.ShapeDtypeStruct((replicas, keep, PART), F32),
        ],
        in_specs=[ANY] * (1 + len(after)),
        out_specs=[VMEM] * 2,
        scratch_shapes=[
            pltpu.VMEM((keep, blocks), jnp.int32),
            pltpu.VMEM((replicas, keep, lanes), jnp.int32),
            pltpu.SemaphoreType.DMA((2,)),
        ],
        compiler_params=pltpu.CompilerParams(vmem_limit_bytes=limit),
        cost_estimate=COST,
    )(kept_index, *after)


def select(parts, momentum, half, factor, chosen, forward_cos, kept, after=()):
    before = [] if kept is None else [kept]
    width = momentum.shape[1]
    pairs = width // (2 * BLOCK)

    def kernel(*refs):
        part_refs = refs[: len(parts)]
        momentum_ref, chosen_ref, cos_ref = refs[len(parts) : len(parts) + 3]
        kept_ref, moment_ref, masked_ref = refs[-3:]
        if before:
            kept_ref[: 2 * pairs * HALF // PART] = refs[len(parts) + 3][...]
        bounds = sorted({p[2] for p in parts} | {HALF})
        sums = []
        for low, high in zip(bounds[:-1], bounds[1:]):
            total = None
            for (_, start, at, size), ref in zip(parts, part_refs):
                if at <= low and at + size >= high:
                    piece = ref[start + low - at : start + high - at, :]
                    total = piece if total is None else total + piece
            sums.append(total)
        gradient = sums[0] if len(sums) == 1 else jnp.concatenate(sums, axis=0)
        moment = DECAY * momentum_ref[half * HALF : (half + 1) * HALF, :] + factor * gradient
        moment_ref[...] = moment
        high, low = halves(moment)
        frequency = lax.broadcasted_iota(jnp.int32, (BLOCK, HALF), 0).astype(F32)
        for g in range(pairs):
            columns = slice(2 * BLOCK * g, 2 * BLOCK * (g + 1))
            values = jnp.concatenate([high[:, columns], low[:, columns], high[:, columns]], axis=1)
            spectrum = lax.dot_general(cos_ref[...], values, (((1,), (1,)), ((), ())), preferred_element_type=F32)
            for s in range(2):
                own = spectrum[s * BLOCK : (s + 1) * BLOCK]
                c = 2 * g + s
                filled = jnp.zeros_like(own)
                for j in range(KEEP):
                    hit = frequency == chosen_ref[c, j : j + 1, half * HALF : (half + 1) * HALF]
                    taken = jnp.where(hit, own, 0.0)
                    kept = jnp.sum(taken, axis=0, keepdims=True)
                    for p in range(HALF // PART):
                        at = (len(before) * HALF // PART + p) * 2 * pairs + c
                        kept_ref[at, j : j + 1, :] = kept[:, p * PART : (p + 1) * PART]
                    filled = filled + taken
                masked_ref[c * BLOCK : (c + 1) * BLOCK, :] = filled

    return pl.pallas_call(
        kernel,
        out_shape=[
            jax.ShapeDtypeStruct((2 * pairs * HALF // PART * (1 + len(before)), KEEP, PART), F32),
            jax.ShapeDtypeStruct((HALF, width), F32),
            jax.ShapeDtypeStruct((width, HALF), F32),
        ],
        in_specs=[VMEM] * (len(parts) + 3 + len(before)) + [ANY] * len(after),
        out_specs=[VMEM] * 3,
        compiler_params=pltpu.CompilerParams(vmem_limit_bytes=24 << 20),
        cost_estimate=COST,
    )(*[p[0] for p in parts], momentum, chosen, forward_cos, *before, *after)


def inverse_of(spectra, inverse_cos):
    high, low = halves(spectra)
    return lax.dot_general(
        jnp.concatenate([high, low, high], axis=0), inverse_cos, (((0,), (0,)), ((), ())), preferred_element_type=F32
    )


def remain(moments, masked, inverse_cos, after=()):
    width = moments[0].shape[1]

    def kernel(*refs):
        cos = refs[4][...]
        out_ref = refs[-1]
        for half in range(2):
            for g in range(width // PART):
                columns = slice(PART * g, PART * (g + 1))
                rebuilt = inverse_of(refs[2 + half][columns, :], cos)
                out_ref[half * HALF : (half + 1) * HALF, columns] = refs[half][:, columns] - rebuilt

    return pl.pallas_call(
        kernel,
        out_shape=jax.ShapeDtypeStruct((2 * HALF, width), F32),
        grid=(1,),
        in_specs=[VMEM] * 5 + [ANY] * len(after),
        out_specs=pl.BlockSpec((2 * HALF, width), lambda i: (0, 0)),
        compiler_params=pltpu.CompilerParams(vmem_limit_bytes=24 << 20),
        cost_estimate=COST,
    )(*moments, *masked, inverse_cos, *after)


def spread(values, chosen, copies):
    members, keep, rows = values.shape

    def kernel(value_ref, chosen_ref, out_ref):
        frequency = lax.broadcasted_iota(jnp.int32, (BLOCK, rows), 0).astype(F32)

        def add(m, total):
            replica = m // (NC * NZ) * (NC * NZ) + m % NZ * NC + m // NZ % NC
            own = jnp.zeros((BLOCK, rows), F32)
            for j in range(keep):
                hit = frequency == chosen_ref[replica, j : j + 1, :]
                own = jnp.where(hit, value_ref[m, j : j + 1, :], own)
            return total + own

        total = lax.fori_loop(0, members, add, jnp.zeros((BLOCK, rows), F32), unroll=4)
        for i in range(copies):
            out_ref[i] = total

    return pl.pallas_call(
        kernel,
        out_shape=jax.ShapeDtypeStruct((copies, BLOCK, rows), F32),
        in_specs=[VMEM] * 2,
        out_specs=VMEM,
        compiler_params=pltpu.CompilerParams(vmem_limit_bytes=24 << 20),
        cost_estimate=COST,
    )(values, chosen)


def finish(mine, other, inverse_cos, scale):
    width = mine.shape[0] // NH * BLOCK

    def kernel(mine_ref, other_ref, cos_ref, out_ref):
        core = lax.axis_index("replica") % NC
        cos = cos_ref[...]
        for ref, place in ((mine_ref, core), (other_ref, 1 - core)):
            for h in range(NH):
                first = pl.multiple_of((h * NC + place) * PART, PART)
                for g in range(width // PART):
                    at = h * (width // BLOCK) + 2 * g
                    spectra = jnp.concatenate([ref[at], ref[at + 1]], axis=0)
                    out_ref[pl.ds(first, PART), PART * g : PART * (g + 1)] = scale * inverse_of(spectra, cos)

    return pl.pallas_call(
        kernel,
        out_shape=jax.ShapeDtypeStruct((NH * NC * PART, width), F32),
        in_specs=[VMEM] * 3,
        out_specs=VMEM,
        compiler_params=pltpu.CompilerParams(vmem_limit_bytes=24 << 20),
        cost_estimate=COST,
    )(mine, other, inverse_cos)


def on_device(tokens, cotangent, momentum, kept_index):
    group_size = lax.axis_size("fsdp")
    replicas = lax.axis_size("replica")
    factor = 1.0 / math.sqrt(tokens.shape[0] * group_size)
    forward_cos, inverse_cos = (jnp.asarray(m) for m in stacked_cosines())


    up = [(i, i // NY * NY + (i + 1) % NY) for i in range(NX * NY)]
    down = [(i, i // NY * NY + (i - 1) % NY) for i in range(NX * NY)]
    across = [(i, (i + NY) % (NX * NY)) for i in range(NX * NY)]
    to_up = lambda v: lax.ppermute(v, "fsdp", up)
    to_down = lambda v: lax.ppermute(v, "fsdp", down)
    to_across = lambda v: lax.ppermute(v, "fsdp", across)
    to_core = lambda v: lax.ppermute(v, "replica", [(i, i ^ 1) for i in range(replicas)])

    make = functools.partial(products, tokens, cotangent)

    (x21,) = make([(1, 2, 1), (1, 1, 1), (1, 3, 1)], [3], limit=60 << 20)
    rx21 = to_across(x21)
    far0, far1 = make([(0, 2, 0), (1, 2, 0)], [1, 1], limit=57 << 20, after=[x21])
    a1, b1 = to_up(far0), to_down(far1)
    near1, near0 = make([(1, 1, 0), (0, 3, 0)], [1, 1], limit=54 << 20, after=[far0])
    a2, b2 = to_up(near1), to_down(near0)
    last0, last1 = make([(0, 1, 0), (1, 3, 0)], [1, 1], limit=52 << 20, after=[near1])
    own_chosen, all_chosen = sort_index(kept_index, limit=50 << 20, after=[last0])
    last0, last1 = combine([[(HALF, [(last0, 0), (a1, 0)])], [(HALF, [(last1, 0), (b1, 0)])]], after=[own_chosen])
    a3, b3 = to_up(last0), to_down(last1)
    x0, other, own, q2, q1, q3, q0 = make(
        [(1, 0, 1), (1, 0, 0), (0, 0, 0), (0, 2, 1), (0, 1, 1), (0, 3, 1), (0, 0, 1)],
        [1] * 7,
        limit=48 << 20,
        after=[last0],
    )
    rx0 = to_across(x0)
    q2a, q2b = combine(
        [[(PART, [(q2, 0), (rx21, 0)])], [(PART, [(q2, PART), (rx21, PART)])]], after=[own]
    )
    qa1, qb1 = to_up(q2a), to_down(q2b)
    other, own = combine(
        [[(HALF, [(other, 0), (a2, 0), (b3, 0)])], [(HALF, [(own, 0), (b2, 0), (a3, 0)])]], after=[q2a]
    )
    received = to_across(other)
    q1, q3, q0 = combine(
        [
            [(PART, [(q1, 0), (rx21, HALF), (qa1, 0)]), (PART, [(q1, PART), (rx21, HALF + PART)])],
            [(PART, [(q3, 0), (rx21, 2 * HALF)]), (PART, [(q3, PART), (rx21, 2 * HALF + PART), (qb1, 0)])],
            [(HALF, [(q0, 0), (rx0, 0)])],
        ],
        after=[other],
    )
    qa, qb = to_up(q1), to_down(q3)

    pieces0 = [(piece, 0, 0, HALF) for piece in (own, received)]
    pieces1 = [(piece, 0, 0, HALF) for piece in (q0, qa, qb)]
    kept, moment0, masked0 = select(pieces0, momentum[0], 0, factor, own_chosen, forward_cos, None, after=[q0])
    kept, moment1, masked1 = select(pieces1, momentum[0], 1, factor, own_chosen, forward_cos, kept)

    order = [i * NZ * NC + j * NC + k for i in range(NH) for k in range(NC) for j in range(NZ)]
    kept = lax.all_to_all(kept, "replica", 0, 0, tiled=True, axis_index_groups=[order])
    summed = spread(kept, all_chosen, NH * NZ)
    cores = [[i * NZ * NC + j * NC + k for i in range(NH) for j in range(NZ)] for k in range(NC)]
    mine = lax.all_to_all(summed, "replica", 0, 0, tiled=True, axis_index_groups=cores)
    theirs = to_core(mine)
    rest = remain([moment0, moment1], [masked0, masked1], inverse_cos, after=[mine])
    update = finish(mine, theirs, inverse_cos, 1.0 / replicas)
    return rest[None], update


def solution(mesh):
    in_specs = (
        P(("replica", "fsdp"), None),
        P(("replica", "fsdp"), None),
        P("replica", "fsdp", None),
        P(None, None, "fsdp"),
    )
    out_specs = (P("replica", "fsdp", None), P("fsdp", None))
    return jax.shard_map(
        on_device, mesh=mesh, in_specs=in_specs, out_specs=out_specs, check_vma=False
    )
```

time: 123 us -> 117 us (0.951)
  blocking collectives: 17.9 us -> 44.2 us
  starting transfers between devices: 38.7 us -> 19.6 us
  local copies, waits for them, and re-layouts: 10.9 us -> 1.1 us
  Pallas kernels: 24.5 us -> 22.9 us
    all_to_all x1 -> x2, blocking collectives: 17.9 us -> 44.2 us  [the longest x1 25.6 us: on_device(): lax.all_to_all(kept, 'replica', 0, 0, tiled=True, axis_index_groups=[order])]
    ppermute x3, waiting for transfers between devices: 2.29 us -> 17.3 us  [on_device(): to_across = lambda v: lax.ppermute(v, 'fsdp', across)]
    all_to_all x1 -> x0, starting transfers between devices: 13.2 us -> none  [on_device(): lax.all_to_all(kept, 'replica', 0, 0, tiled=True, axis_index_groups=groups)]
    unnamed x42 -> x10, local copies, waits for them, and re-layouts: 10.2 us -> 1.1 us
    all_to_all x1 -> x0, waiting for transfers between devices: 7.28 us -> none  [on_device(): lax.all_to_all(kept, 'replica', 0, 0, tiled=True, axis_index_groups=groups)]
    ppermute x2 -> x1, starting transfers between devices: 6.38 us -> 1.88 us  [on_device(): lax.ppermute(v, 'replica', [(i, i ^ 1) for i in range(replicas)])]
    ppermute x5, waiting for transfers between devices: 14.3 us -> 10.4 us  [on_device(): to_up = lambda v: lax.ppermute(v, 'fsdp', up)]
    ppermute x5, starting transfers between devices: 14.9 us -> 11.7 us  [on_device(): to_down = lambda v: lax.ppermute(v, 'fsdp', down)]
  transfers between devices with their start and end apart: 16 -> 14, of which waited for: 9 -> 9; matrix products, arithmetic and copies ran while one was open for 1% -> 0% of each run, Pallas kernels for 13% -> 14%
where the time goes in v2:
time: 117 us
  blocking collectives  44.2 us (38%)
  waiting for transfers between devices  28.1 us (24%)
  Pallas kernels  22.9 us (20%)
  starting transfers between devices  19.6 us (17%)
    all_to_all x1, blocking collectives, on_device(): lax.all_to_all(kept, 'replica', 0, 0, tiled=True, axis_index_groups=[order])  25.6 us
    all_to_all x1, blocking collectives, on_device(): lax.all_to_all(summed, 'replica', 0, 0, tiled=True, axis_index_groups=cores)  18.6 us
    ppermute x3, waiting for transfers between devices, on_device(): to_across = lambda v: lax.ppermute(v, 'fsdp', across)  17.3 us
    pallas_call x5, Pallas kernels, products(): pl.pallas_call(kernel, out_shape=[jax.ShapeDtypeStruct(s, F32) for s in s...  15.1 us
    ppermute x5, starting transfers between devices, on_device(): to_down = lambda v: lax.ppermute(v, 'fsdp', down)  11.7 us
    ppermute x5, waiting for transfers between devices, on_device(): to_up = lambda v: lax.ppermute(v, 'fsdp', up)  10.4 us
    ppermute x3, starting transfers between devices, on_device(): to_across = lambda v: lax.ppermute(v, 'fsdp', across)  4.74 us
  transfers between devices with their start and end apart: 14, of which 9 were waited for; matrix products, arithmetic and copies ran while one was open for 0% of the time, Pallas kernels for 14%

profile of v2, /device:TPU:1, one launch (start us, length us, event | category | flops | bytes accessed | tf_op | source)
XLA Modules:
  0.0 116.7 jit_solution(11524725031739386463)
XLA Ops:
  0.6 3.6 %shard_map.77.refs_0_ = f32[768,512]{1,0:T(8,128)} custom-call(bf16[640,4096]{1,0:T(8,128)(2,1)} %tokens_ref.9, bf16[640,512]{1,0:T(8,128)(2,1)} %cot_ref.9), custom_call_target="tpu_custom_call" | custom-call | flops 1 | bytes 1 | tf_op jit(solution)/shard_map/pallas_call | solution.py:76
  4.2 2.1 %collective-permute-start.6 = (f32[768,512]{1,0:T(8,128)}, f32[768,512]{1,0:T(8,128)S(1)}, u32[]{:S(2)}, u32[]{:S(2)}) collective-permute-start(f32[768,512]{1,0:T(8,128)} %shard_map.77.refs_0_), channel_id=1, source_target_pairs={{0,4},{1,5},{2,6},{3,7},{4,0},{5,1},{6,2},{7,3},{8,12},{9,13},{10,... | collective-permute-start | bytes 4718600 | tf_op jit(solution)/shard_map/ppermute | solution.py:329
  6.3 2.8 %shard_map.78 = (f32[256,512]{1,0:T(8,128)}, f32[256,512]{1,0:T(8,128)}) custom-call(bf16[640,4096]{1,0:T(8,128)(2,1)} %tokens_ref.9, bf16[640,512]{1,0:T(8,128)(2,1)} %cot_ref.9, f32[768,512]{1,0:T(8,128)} %shard_map.77.refs_0_), custom_call_target="tpu_custom_call" | custom-call | flops 1 | bytes 1 | tf_op jit(solution)/shard_map/pallas_call | solution.py:76
  9.1 2.8 %collective-permute-start.1 = (f32[256,512]{1,0:T(8,128)}, f32[256,512]{1,0:T(8,128)S(1)}, u32[]{:S(2)}, u32[]{:S(2)}) collective-permute-start(f32[256,512]{1,0:T(8,128)} %get-tuple-element.36), channel_id=1, source_target_pairs={{0,3},{1,0},{2,1},{3,2},{4,7},{5,4},{6,5},{7,6},{8,11},{9,8},{10,9... | collective-permute-start | bytes 1572872 | tf_op jit(solution)/shard_map/ppermute | solution.py:328
  11.9 2.8 %shard_map.79 = (f32[256,512]{1,0:T(8,128)}, f32[256,512]{1,0:T(8,128)}) custom-call(bf16[640,4096]{1,0:T(8,128)(2,1)} %tokens_ref.9, bf16[640,512]{1,0:T(8,128)(2,1)} %cot_ref.9, f32[256,512]{1,0:T(8,128)} %get-tuple-element.32.refs_0_), custom_call_target="tpu_custom_call" | custom-call | flops 1 | bytes 1 | tf_op jit(solution)/shard_map/pallas_call | solution.py:76
  14.7 2.8 %collective-permute-start.4 = (f32[256,512]{1,0:T(8,128)}, f32[256,512]{1,0:T(8,128)S(1)}, u32[]{:S(2)}, u32[]{:S(2)}) collective-permute-start(f32[256,512]{1,0:T(8,128)} %get-tuple-element.42), channel_id=1, source_target_pairs={{0,3},{1,0},{2,1},{3,2},{4,7},{5,4},{6,5},{7,6},{8,11},{9,8},{10,9... | collective-permute-start | bytes 1572872 | tf_op jit(solution)/shard_map/ppermute | solution.py:328
  17.5 1.1 copy-done.2
  18.5 2.0 %shard_map.80 = (f32[256,512]{1,0:T(8,128)S(1)}, f32[256,512]{1,0:T(8,128)S(1)}) custom-call(bf16[640,4096]{1,0:T(8,128)(2,1)} %tokens_ref.9, bf16[640,512]{1,0:T(8,128)(2,1)} %cot_ref.9, f32[256,512]{1,0:T(8,128)S(1)} %copy-done.2), custom_call_target="tpu_custom_call" | custom-call | flops 1 | bytes 1 | tf_op jit(solution)/shard_map/pallas_call | solution.py:76
  20.5 1.7 %shard_map.81 = (f32[8,8,512]{2,1,0:T(8,128)S(1)}, f32[32,8,128]{2,1,0:T(8,128)S(1)}) custom-call(s32[32,8,4096]{2,1,0:T(8,128)} %index_ref.1, f32[256,512]{1,0:T(8,128)S(1)} %get-tuple-element.34.refs_0_), custom_call_target="tpu_custom_call" | custom-call | flops 1 | bytes 1 | tf_op jit(solution)/shard_map/pallas_call | solution.py:160
  22.2 0.3 collective-permute-done.1.refs_3_
  22.5 3.0 %collective-permute-done.refs_1_ = f32[256,512]{1,0:T(8,128)S(1)} collective-permute-done((f32[256,512]{1,0:T(8,128)}, f32[256,512]{1,0:T(8,128)S(1)}, u32[]{:S(2)}, u32[]{:S(2)}) %collective-permute-start) | collective-permute-done | bytes 524320 | tf_op jit(solution)/shard_map/ppermute | solution.py:327
  25.6 0.4 collective-permute-start.3
  26.0 1.2 collective-permute-start.5
  27.2 4.0 %shard_map.83 = (f32[256,512]{1,0:T(8,128)S(1)}, f32[256,512]{1,0:T(8,128)S(1)}, f32[256,512]{1,0:T(8,128)S(1)}, f32[256,512]{1,0:T(8,128)S(1)}, f32[256,512]{1,...) custom-call(bf16[640,4096]{1,0:T(8,128)(2,1)} %tokens_ref.9, bf16[640,512]{1,0:T(8,128)(2,1)S(1)} %copy-done, ...), custom_call_target="tpu_custom_call" | custom-call | flops 1 | bytes 1 | tf_op jit(solution)/shard_map/pallas_call | solution.py:76
  31.2 8.3 %collective-permute-done.6.refs_1_ = f32[768,512]{1,0:T(8,128)S(1)} collective-permute-done((f32[768,512]{1,0:T(8,128)}, f32[768,512]{1,0:T(8,128)S(1)}, u32[]{:S(2)}, u32[]{:S(2)}) %collective-permute-start.6) | collective-permute-done | bytes 1572896 | tf_op jit(solution)/shard_map/ppermute | solution.py:329
  39.4 2.1 %collective-permute-start.10 = (f32[256,512]{1,0:T(8,128)S(1)}, f32[256,512]{1,0:T(8,128)S(1)}, u32[]{:S(2)}, u32[]{:S(2)}) collective-permute-start(f32[256,512]{1,0:T(8,128)S(1)} %get-tuple-element.51), channel_id=1, source_target_pairs={{0,4},{1,5},{2,6},{3,7},{4,0},{5,1},{6,2},{7,3},{8,12},{9,13},{10,... | collective-permute-start | bytes 1572872 | tf_op jit(solution)/shard_map/ppermute | solution.py:329
  41.6 3.1 %collective-permute-start.9 = (f32[128,512]{1,0:T(8,128)S(1)}, f32[128,512]{1,0:T(8,128)S(1)}, u32[]{:S(2)}, u32[]{:S(2)}) collective-permute-start(f32[128,512]{1,0:T(8,128)S(1)} %get-tuple-element.49), channel_id=1, source_target_pairs={{0,3},{1,0},{2,1},{3,2},{4,7},{5,4},{6,5},{7,6},{8,11},{9,8},{10,9... | collective-permute-start | bytes 786440 | tf_op jit(solution)/shard_map/ppermute | solution.py:328
  44.9 3.1 %collective-permute-done.5.refs_5_ = f32[256,512]{1,0:T(8,128)S(1)} collective-permute-done((f32[256,512]{1,0:T(8,128)S(1)}, f32[256,512]{1,0:T(8,128)S(1)}, u32[]{:S(2)}, u32[]{:S(2)}) %collective-permute-start.5) | collective-permute-done | bytes 524320 | tf_op jit(solution)/shard_map/ppermute | solution.py:327
  48.1 0.5 collective-permute-start.7
  48.7 3.0 %collective-permute-done.10.refs_6_ = f32[256,512]{1,0:T(8,128)S(1)} collective-permute-done((f32[256,512]{1,0:T(8,128)S(1)}, f32[256,512]{1,0:T(8,128)S(1)}, u32[]{:S(2)}, u32[]{:S(2)}) %collective-permute-start.10) | collective-permute-done | bytes 524320 | tf_op jit(solution)/shard_map/ppermute | solution.py:329
  51.6 2.2 %collective-permute-done.8.refs_2_ = f32[128,512]{1,0:T(8,128)S(1)} collective-permute-done((f32[128,512]{1,0:T(8,128)S(1)}, f32[128,512]{1,0:T(8,128)S(1)}, u32[]{:S(2)}, u32[]{:S(2)}) %collective-permute-start.8) | collective-permute-done | bytes 262176 | tf_op jit(solution)/shard_map/ppermute | solution.py:327
  54.1 2.7 %collective-permute-start.12 = (f32[256,512]{1,0:T(8,128)S(1)}, f32[256,512]{1,0:T(8,128)S(1)}, u32[]{:S(2)}, u32[]{:S(2)}) collective-permute-start(f32[256,512]{1,0:T(8,128)S(1)} %get-tuple-element.55), channel_id=1, source_target_pairs={{0,3},{1,0},{2,1},{3,2},{4,7},{5,4},{6,5},{7,6},{8,11},{9,8},{10,9... | collective-permute-start | bytes 1572872 | tf_op jit(solution)/shard_map/ppermute | solution.py:328
  56.8 6.1 %collective-permute-done.7.refs_1_ = f32[256,512]{1,0:T(8,128)S(1)} collective-permute-done((f32[256,512]{1,0:T(8,128)S(1)}, f32[256,512]{1,0:T(8,128)S(1)}, u32[]{:S(2)}, u32[]{:S(2)}) %collective-permute-start.7) | collective-permute-done | bytes 524320 | tf_op jit(solution)/shard_map/ppermute | solution.py:329
  62.9 0.9 shard_map.87
  63.8 2.1 %collective-permute-done.11.refs_1_ = f32[256,512]{1,0:T(8,128)S(1)} collective-permute-done((f32[256,512]{1,0:T(8,128)S(1)}, f32[256,512]{1,0:T(8,128)S(1)}, u32[]{:S(2)}, u32[]{:S(2)}) %collective-permute-start.11) | collective-permute-done | bytes 524320 | tf_op jit(solution)/shard_map/ppermute | solution.py:327
  65.8 0.9 shard_map.88
  66.7 25.6 %all_to_all.10.value_ref = f32[32,8,128]{2,1,0:T(8,128)S(1)} all-to-all(f32[32,8,128]{2,1,0:T(8,128)S(1)} %get-tuple-element.60), channel_id=1, replica_groups={{0,16,32,48,64,80,96,112,8,24,40,56,72,88,104,120,128,144,160,176,192,2..., dimensions={0} | all-to-all | bytes 262144 | tf_op jit(solution)/shard_map/all_to_all | solution.py:375
  92.3 0.7 shard_map.89
  93.1 18.6 %all_to_all.11.refs_5_.mine_ref = f32[16,64,128]{2,1,0:T(8,128)S(1)} all-to-all(f32[16,64,128]{2,1,0:T(8,128)S(1)} %shard_map.89), channel_id=1, replica_groups={{0,16,32,48,64,80,96,112,128,144,160,176,192,208,224,240},{8,24,40,56,7..., dimensions={0} | all-to-all | bytes 1048576 | tf_op jit(solution)/shard_map/all_to_all | solution.py:378
  111.7 1.9 %collective-permute-start.13 = (f32[16,64,128]{2,1,0:T(8,128)S(1)}, f32[16,64,128]{2,1,0:T(8,128)S(1)}, u32[]{:S(2)}, u32[]{:S(2)}) collective-permute-start(f32[16,64,128]{2,1,0:T(8,128)S(1)} %all_to_all.11.refs_5_.mine_ref), channel_id=1, source_target_pairs={{0,8},{8,0},{16,24},{24,16},{32,40},{40,32},{48,56},{56,48},{64,72... | collective-permute-start | bytes 1572872 | tf_op jit(solution)/shard_map/ppermute | solution.py:330
  113.6 1.6 %shard_map.90 = f32[512,512]{1,0:T(8,128)} custom-call(f32[256,512]{1,0:T(8,128)S(1)} %get-tuple-element.53.refs_0_, f32[256,512]{1,0:T(8,128)S(1)} %get-tuple-element.57.refs_1_, f32[512,256]{1,0:T(8,128)S(1)} %get-tuple-element.58.refs_2_, f32[512,256]{1,0:T(8,128)S(1)} %get-tuple-element.59.refs_3_, bf16[384,128]{1,0:T(8,128)(2,1)S(1)} %copy-done.4, ...), custom_call_target="tpu_custom_call" | custom-call | flops 1 | bytes 1 | tf_op jit(solution)/shard_map/pallas_call | solution.py:254
  115.1 1.6 %shard_map.91 = f32[512,512]{1,0:T(8,128)} custom-call(f32[16,64,128]{2,1,0:T(8,128)S(1)} %all_to_all.11.refs_5_.mine_ref, f32[16,64,128]{2,1,0:T(8,128)S(1)} %collective-permute-done.13.other_ref, bf16[384,128]{1,0:T(8,128)(2,1)S(1)} %copy-done.4), custom_call_target="tpu_custom_call" | custom-call | flops 1 | bytes 1 | tf_op jit(solution)/shard_map/pallas_call | solution.py:307
  (23 shorter events, 0.8 us)
Async XLA Ops:
  4.2 35.2 %collective-permute-start.6 = (f32[768,512]{1,0:T(8,128)}, f32[768,512]{1,0:T(8,128)S(1)}, u32[]{:S(2)}, u32[]{:S(2)}) collective-permute-start(f32[768,512]{1,0:T(8,128)} %shard_map.77.refs_0_), channel_id=1, source_target_pairs={{0,4},{1,5},{2,6},{3,7},{4,0},{5,1},{6,2},{7,3},{8,12},{9,13},{10,... | collective-permute-start | bytes 4718600 | tf_op jit(solution)/shard_map/ppermute | solution.py:329
  9.1 13.4 %collective-permute-start.1 = (f32[256,512]{1,0:T(8,128)}, f32[256,512]{1,0:T(8,128)S(1)}, u32[]{:S(2)}, u32[]{:S(2)}) collective-permute-start(f32[256,512]{1,0:T(8,128)} %get-tuple-element.36), channel_id=1, source_target_pairs={{0,3},{1,0},{2,1},{3,2},{4,7},{5,4},{6,5},{7,6},{8,11},{9,8},{10,9... | collective-permute-start | bytes 1572872 | tf_op jit(solution)/shard_map/ppermute | solution.py:328
  11.9 13.6 %collective-permute-start = (f32[256,512]{1,0:T(8,128)}, f32[256,512]{1,0:T(8,128)S(1)}, u32[]{:S(2)}, u32[]{:S(2)}) collective-permute-start(f32[256,512]{1,0:T(8,128)} %get-tuple-element.32.refs_0_), channel_id=1, source_target_pairs={{0,1},{1,2},{2,3},{3,0},{4,5},{5,6},{6,7},{7,4},{8,9},{9,10},{10,1... | collective-permute-start | bytes 1572872 | tf_op jit(solution)/shard_map/ppermute | solution.py:327
  14.7 26.9 %collective-permute-start.4 = (f32[256,512]{1,0:T(8,128)}, f32[256,512]{1,0:T(8,128)S(1)}, u32[]{:S(2)}, u32[]{:S(2)}) collective-permute-start(f32[256,512]{1,0:T(8,128)} %get-tuple-element.42), channel_id=1, source_target_pairs={{0,3},{1,0},{2,1},{3,2},{4,7},{5,4},{6,5},{7,6},{8,11},{9,8},{10,9... | collective-permute-start | bytes 1572872 | tf_op jit(solution)/shard_map/ppermute | solution.py:328
  17.5 27.2 %collective-permute-start.2 = (f32[256,512]{1,0:T(8,128)}, f32[256,512]{1,0:T(8,128)S(1)}, u32[]{:S(2)}, u32[]{:S(2)}) collective-permute-start(f32[256,512]{1,0:T(8,128)} %get-tuple-element.33.refs_0_), channel_id=1, source_target_pairs={{0,1},{1,2},{2,3},{3,0},{4,5},{5,6},{6,7},{7,4},{8,9},{9,10},{10,1... | collective-permute-start | bytes 1572872 | tf_op jit(solution)/shard_map/ppermute | solution.py:327
  17.5 1.1 copy-start.2
  20.5 6.6 %copy-start = (bf16[640,512]{1,0:T(8,128)(2,1)S(1)}, bf16[640,512]{1,0:T(8,128)(2,1)}, u32[]{:S(2)}) copy-start(bf16[640,512]{1,0:T(8,128)(2,1)} %cot_ref.9) | copy-start | bytes 1966084
  25.6 19.2 %collective-permute-start.3 = (f32[256,512]{1,0:T(8,128)S(1)}, f32[256,512]{1,0:T(8,128)S(1)}, u32[]{:S(2)}, u32[]{:S(2)}) collective-permute-start(f32[256,512]{1,0:T(8,128)S(1)} %get-tuple-element.40), channel_id=1, source_target_pairs={{0,3},{1,0},{2,1},{3,2},{4,7},{5,4},{6,5},{7,6},{8,11},{9,8},{10,9... | collective-permute-start | bytes 1572872 | tf_op jit(solution)/shard_map/ppermute | solution.py:328
  26.0 22.0 %collective-permute-start.5 = (f32[256,512]{1,0:T(8,128)S(1)}, f32[256,512]{1,0:T(8,128)S(1)}, u32[]{:S(2)}, u32[]{:S(2)}) collective-permute-start(f32[256,512]{1,0:T(8,128)S(1)} %get-tuple-element.38.refs_0_), channel_id=1, source_target_pairs={{0,1},{1,2},{2,3},{3,0},{4,5},{5,6},{6,7},{7,4},{8,9},{9,10},{10,1... | collective-permute-start | bytes 1572872 | tf_op jit(solution)/shard_map/ppermute | solution.py:327
  39.4 12.2 %collective-permute-start.10 = (f32[256,512]{1,0:T(8,128)S(1)}, f32[256,512]{1,0:T(8,128)S(1)}, u32[]{:S(2)}, u32[]{:S(2)}) collective-permute-start(f32[256,512]{1,0:T(8,128)S(1)} %get-tuple-element.51), channel_id=1, source_target_pairs={{0,4},{1,5},{2,6},{3,7},{4,0},{5,1},{6,2},{7,3},{8,12},{9,13},{10,... | collective-permute-start | bytes 1572872 | tf_op jit(solution)/shard_map/ppermute | solution.py:329
  41.6 21.3 %copy-start.1 = (f32[1,512,512]{2,1,0:T(8,128)S(1)}, f32[1,512,512]{2,1,0:T(8,128)}, u32[]{:S(2)}) copy-start(f32[1,512,512]{2,1,0:T(8,128)} %param.8) | copy-start | bytes 3145732
  41.6 21.3 %copy-start.3 = (bf16[128,384]{1,0:T(8,128)(2,1)S(1)}, bf16[128,384]{1,0:T(8,128)(2,1)}, u32[]{:S(2)}) copy-start(bf16[128,384]{1,0:T(8,128)(2,1)} %constant.4.clone.refs_4_.refs_5_) | copy-start | bytes 294916
  41.6 10.0 %collective-permute-start.9 = (f32[128,512]{1,0:T(8,128)S(1)}, f32[128,512]{1,0:T(8,128)S(1)}, u32[]{:S(2)}, u32[]{:S(2)}) collective-permute-start(f32[128,512]{1,0:T(8,128)S(1)} %get-tuple-element.49), channel_id=1, source_target_pairs={{0,3},{1,0},{2,1},{3,2},{4,7},{5,4},{6,5},{7,6},{8,11},{9,8},{10,9... | collective-permute-start | bytes 786440 | tf_op jit(solution)/shard_map/ppermute | solution.py:328
  44.7 9.1 %collective-permute-start.8 = (f32[128,512]{1,0:T(8,128)S(1)}, f32[128,512]{1,0:T(8,128)S(1)}, u32[]{:S(2)}, u32[]{:S(2)}) collective-permute-start(f32[128,512]{1,0:T(8,128)S(1)} %get-tuple-element.44.refs_6_), channel_id=1, source_target_pairs={{0,1},{1,2},{2,3},{3,0},{4,5},{5,6},{6,7},{7,4},{8,9},{9,10},{10,1... | collective-permute-start | bytes 786440 | tf_op jit(solution)/shard_map/ppermute | solution.py:327
  48.1 14.7 %collective-permute-start.7 = (f32[256,512]{1,0:T(8,128)S(1)}, f32[256,512]{1,0:T(8,128)S(1)}, u32[]{:S(2)}, u32[]{:S(2)}) collective-permute-start(f32[256,512]{1,0:T(8,128)S(1)} %get-tuple-element.46.refs_7_), channel_id=1, source_target_pairs={{0,4},{1,5},{2,6},{3,7},{4,0},{5,1},{6,2},{7,3},{8,12},{9,13},{10,... | collective-permute-start | bytes 1572872 | tf_op jit(solution)/shard_map/ppermute | solution.py:329
  54.0 59.5 %copy-start.4 = (bf16[384,128]{1,0:T(8,128)(2,1)S(1)}, bf16[384,128]{1,0:T(8,128)(2,1)}, u32[]{:S(2)}) copy-start(bf16[384,128]{1,0:T(8,128)(2,1)} %constant.5.clone.refs_4_.cos_ref) | copy-start | bytes 294916
  54.1 11.8 %collective-permute-start.11 = (f32[256,512]{1,0:T(8,128)S(1)}, f32[256,512]{1,0:T(8,128)S(1)}, u32[]{:S(2)}, u32[]{:S(2)}) collective-permute-start(f32[256,512]{1,0:T(8,128)S(1)} %get-tuple-element.54), channel_id=1, source_target_pairs={{0,1},{1,2},{2,3},{3,0},{4,5},{5,6},{6,7},{7,4},{8,9},{9,10},{10,1... | collective-permute-start | bytes 1572872 | tf_op jit(solution)/shard_map/ppermute | solution.py:327
  54.1 11.7 %collective-permute-start.12 = (f32[256,512]{1,0:T(8,128)S(1)}, f32[256,512]{1,0:T(8,128)S(1)}, u32[]{:S(2)}, u32[]{:S(2)}) collective-permute-start(f32[256,512]{1,0:T(8,128)S(1)} %get-tuple-element.55), channel_id=1, source_target_pairs={{0,3},{1,0},{2,1},{3,2},{4,7},{5,4},{6,5},{7,6},{8,11},{9,8},{10,9... | collective-permute-start | bytes 1572872 | tf_op jit(solution)/shard_map/ppermute | solution.py:328
  111.7 3.5 %collective-permute-start.13 = (f32[16,64,128]{2,1,0:T(8,128)S(1)}, f32[16,64,128]{2,1,0:T(8,128)S(1)}, u32[]{:S(2)}, u32[]{:S(2)}) collective-permute-start(f32[16,64,128]{2,1,0:T(8,128)S(1)} %all_to_all.11.refs_5_.mine_ref), channel_id=1, source_target_pairs={{0,8},{8,0},{16,24},{24,16},{32,40},{40,32},{48,56},{56,48},{64,72... | collective-permute-start | bytes 1572872 | tf_op jit(solution)/shard_map/ppermute | solution.py:330

commit v3 on v2

--- a/solution.py
+++ b/solution.py
@@ -331,9 +331,8 @@
 
     make = functools.partial(products, tokens, cotangent)
 
-    (x21,) = make([(1, 2, 1), (1, 1, 1), (1, 3, 1)], [3], limit=60 << 20)
+    x21, far0, far1 = make([(1, 2, 1), (1, 1, 1), (1, 3, 1), (0, 2, 0), (1, 2, 0)], [3, 1, 1], limit=60 << 20)
     rx21 = to_across(x21)
-    far0, far1 = make([(0, 2, 0), (1, 2, 0)], [1, 1], limit=57 << 20, after=[x21])
     a1, b1 = to_up(far0), to_down(far1)
     near1, near0 = make([(1, 1, 0), (0, 3, 0)], [1, 1], limit=54 << 20, after=[far0])
     a2, b2 = to_up(near1), to_down(near0)
@@ -356,15 +355,18 @@
         [[(HALF, [(other, 0), (a2, 0), (b3, 0)])], [(HALF, [(own, 0), (b2, 0), (a3, 0)])]], after=[q2a]
     )
     received = to_across(other)
-    q1, q3, q0 = combine(
+    (q1,) = combine(
+        [[(PART, [(q1, 0), (rx21, HALF), (qa1, 0)]), (PART, [(q1, PART), (rx21, HALF + PART)])]], after=[other]
+    )
+    qa = to_up(q1)
+    q3, q0 = combine(
         [
-            [(PART, [(q1, 0), (rx21, HALF), (qa1, 0)]), (PART, [(q1, PART), (rx21, HALF + PART)])],
             [(PART, [(q3, 0), (rx21, 2 * HALF)]), (PART, [(q3, PART), (rx21, 2 * HALF + PART), (qb1, 0)])],
             [(HALF, [(q0, 0), (rx0, 0)])],
         ],
-        after=[other],
-    )
-    qa, qb = to_up(q1), to_down(q3)
+        after=[q1],
+    )
+    qb = to_down(q3)
 
     pieces0 = [(piece, 0, 0, HALF) for piece in (own, received)]
     pieces1 = [(piece, 0, 0, HALF) for piece in (q0, qa, qb)]

time: 117 us -> 116 us (level)
  Pallas kernels: 22.9 us -> 20.9 us
    pallas_call x5 -> x4, Pallas kernels: 15.1 us -> 13 us  [products(): pl.pallas_call(kernel, out_shape=[jax.ShapeDtypeStruct(s, F32) for s in s...]
    ppermute x5, starting transfers between devices: 1.26 us -> 2.91 us  [on_device(): to_up = lambda v: lax.ppermute(v, 'fsdp', up)]
    ppermute x3, waiting for transfers between devices: 17.3 us -> 18.9 us  [on_device(): to_across = lambda v: lax.ppermute(v, 'fsdp', across)]
    ppermute x5, waiting for transfers between devices: 10.4 us -> 9.2 us  [on_device(): to_up = lambda v: lax.ppermute(v, 'fsdp', up)]
  transfers between devices with their start and end apart: 14 -> 14, of which waited for: 9 -> 8; matrix products, arithmetic and copies ran while one was open for 0% -> 0% of each run, Pallas kernels for 14% -> 12%
where the time goes in v3:
time: 116 us
  blocking collectives  43.9 us (38%)
  waiting for transfers between devices  28.3 us (24%)
  Pallas kernels  20.9 us (18%)
  starting transfers between devices  20.6 us (18%)
    all_to_all x1, blocking collectives, on_device(): lax.all_to_all(kept, 'replica', 0, 0, tiled=True, axis_index_groups=[order])  25.4 us
    ppermute x3, waiting for transfers between devices, on_device(): to_across = lambda v: lax.ppermute(v, 'fsdp', across)  18.9 us
    all_to_all x1, blocking collectives, on_device(): lax.all_to_all(summed, 'replica', 0, 0, tiled=True, axis_index_groups=cores)  18.6 us
    pallas_call x4, Pallas kernels, products(): pl.pallas_call(kernel, out_shape=[jax.ShapeDtypeStruct(s, F32) for s in s...  13 us
    ppermute x5, starting transfers between devices, on_device(): to_down = lambda v: lax.ppermute(v, 'fsdp', down)  11 us
    ppermute x5, waiting for transfers between devices, on_device(): to_up = lambda v: lax.ppermute(v, 'fsdp', up)  9.2 us
    ppermute x3, starting transfers between devices, on_device(): to_across = lambda v: lax.ppermute(v, 'fsdp', across)  4.75 us
    ppermute x5, starting transfers between devices, on_device(): to_up = lambda v: lax.ppermute(v, 'fsdp', up)  2.91 us
  transfers between devices with their start and end apart: 14, of which 8 were waited for; matrix products, arithmetic and copies ran while one was open for 0% of the time, Pallas kernels for 12%

profile of v3, /device:TPU:1, one launch (start us, length us, event | category | flops | bytes accessed | tf_op | source)
XLA Modules:
  0.0 115.6 jit_solution(13387727101453915774)
XLA Ops:
  0.6 4.3 %shard_map.77 = (f32[768,512]{1,0:T(8,128)}, f32[256,512]{1,0:T(8,128)}, f32[256,512]{1,0:T(8,128)}) custom-call(bf16[640,4096]{1,0:T(8,128)(2,1)} %tokens_ref.7, bf16[640,512]{1,0:T(8,128)(2,1)} %cot_ref.7), custom_call_target="tpu_custom_call" | custom-call | flops 1 | bytes 1 | tf_op jit(solution)/shard_map/pallas_call | solution.py:76
  4.9 2.1 %collective-permute-start.6 = (f32[768,512]{1,0:T(8,128)}, f32[768,512]{1,0:T(8,128)S(1)}, u32[]{:S(2)}, u32[]{:S(2)}) collective-permute-start(f32[768,512]{1,0:T(8,128)} %get-tuple-element.44), channel_id=1, source_target_pairs={{0,4},{1,5},{2,6},{3,7},{4,0},{5,1},{6,2},{7,3},{8,12},{9,13},{10,... | collective-permute-start | bytes 4718600 | tf_op jit(solution)/shard_map/ppermute | solution.py:329
  7.1 2.7 %collective-permute-start.1 = (f32[256,512]{1,0:T(8,128)}, f32[256,512]{1,0:T(8,128)S(1)}, u32[]{:S(2)}, u32[]{:S(2)}) collective-permute-start(f32[256,512]{1,0:T(8,128)} %get-tuple-element.36), channel_id=1, source_target_pairs={{0,3},{1,0},{2,1},{3,2},{4,7},{5,4},{6,5},{7,6},{8,11},{9,8},{10,9... | collective-permute-start | bytes 1572872 | tf_op jit(solution)/shard_map/ppermute | solution.py:328
  9.8 2.8 %shard_map.78 = (f32[256,512]{1,0:T(8,128)}, f32[256,512]{1,0:T(8,128)}) custom-call(bf16[640,4096]{1,0:T(8,128)(2,1)} %tokens_ref.7, bf16[640,512]{1,0:T(8,128)(2,1)} %cot_ref.7, f32[256,512]{1,0:T(8,128)} %get-tuple-element.32.refs_0_), custom_call_target="tpu_custom_call" | custom-call | flops 1 | bytes 1 | tf_op jit(solution)/shard_map/pallas_call | solution.py:76
  12.6 2.8 %collective-permute-start.4 = (f32[256,512]{1,0:T(8,128)}, f32[256,512]{1,0:T(8,128)S(1)}, u32[]{:S(2)}, u32[]{:S(2)}) collective-permute-start(f32[256,512]{1,0:T(8,128)} %get-tuple-element.42), channel_id=1, source_target_pairs={{0,3},{1,0},{2,1},{3,2},{4,7},{5,4},{6,5},{7,6},{8,11},{9,8},{10,9... | collective-permute-start | bytes 1572872 | tf_op jit(solution)/shard_map/ppermute | solution.py:328
  15.3 1.1 copy-done.2
  16.4 2.0 %shard_map.79 = (f32[256,512]{1,0:T(8,128)S(1)}, f32[256,512]{1,0:T(8,128)S(1)}) custom-call(bf16[640,4096]{1,0:T(8,128)(2,1)} %tokens_ref.7, bf16[640,512]{1,0:T(8,128)(2,1)} %cot_ref.7, f32[256,512]{1,0:T(8,128)S(1)} %copy-done.2), custom_call_target="tpu_custom_call" | custom-call | flops 1 | bytes 1 | tf_op jit(solution)/shard_map/pallas_call | solution.py:76
  18.4 1.7 %shard_map.80 = (f32[8,8,512]{2,1,0:T(8,128)S(1)}, f32[32,8,128]{2,1,0:T(8,128)S(1)}) custom-call(s32[32,8,4096]{2,1,0:T(8,128)} %index_ref.1, f32[256,512]{1,0:T(8,128)S(1)} %get-tuple-element.34.refs_0_), custom_call_target="tpu_custom_call" | custom-call | flops 1 | bytes 1 | tf_op jit(solution)/shard_map/pallas_call | solution.py:160
  20.1 0.3 collective-permute-done.1.refs_3_
  20.4 3.0 %collective-permute-done.refs_1_ = f32[256,512]{1,0:T(8,128)S(1)} collective-permute-done((f32[256,512]{1,0:T(8,128)}, f32[256,512]{1,0:T(8,128)S(1)}, u32[]{:S(2)}, u32[]{:S(2)}) %collective-permute-start) | collective-permute-done | bytes 524320 | tf_op jit(solution)/shard_map/ppermute | solution.py:327
  23.5 0.4 collective-permute-start.3
  23.9 1.2 %collective-permute-start.5 = (f32[256,512]{1,0:T(8,128)S(1)}, f32[256,512]{1,0:T(8,128)S(1)}, u32[]{:S(2)}, u32[]{:S(2)}) collective-permute-start(f32[256,512]{1,0:T(8,128)S(1)} %get-tuple-element.38.refs_0_), channel_id=1, source_target_pairs={{0,1},{1,2},{2,3},{3,0},{4,5},{5,6},{6,7},{7,4},{8,9},{9,10},{10,1... | collective-permute-start | bytes 1572872 | tf_op jit(solution)/shard_map/ppermute | solution.py:327
  25.0 4.0 %shard_map.82 = (f32[256,512]{1,0:T(8,128)S(1)}, f32[256,512]{1,0:T(8,128)S(1)}, f32[256,512]{1,0:T(8,128)S(1)}, f32[256,512]{1,0:T(8,128)S(1)}, f32[256,512]{1,...) custom-call(bf16[640,4096]{1,0:T(8,128)(2,1)} %tokens_ref.7, bf16[640,512]{1,0:T(8,128)(2,1)S(1)} %copy-done, ...), custom_call_target="tpu_custom_call" | custom-call | flops 1 | bytes 1 | tf_op jit(solution)/shard_map/pallas_call | solution.py:76
  29.0 11.1 %collective-permute-done.6.refs_1_ = f32[768,512]{1,0:T(8,128)S(1)} collective-permute-done((f32[768,512]{1,0:T(8,128)}, f32[768,512]{1,0:T(8,128)S(1)}, u32[]{:S(2)}, u32[]{:S(2)}) %collective-permute-start.6) | collective-permute-done | bytes 1572896 | tf_op jit(solution)/shard_map/ppermute | solution.py:329
  40.1 2.1 %collective-permute-start.9 = (f32[256,512]{1,0:T(8,128)S(1)}, f32[256,512]{1,0:T(8,128)S(1)}, u32[]{:S(2)}, u32[]{:S(2)}) collective-permute-start(f32[256,512]{1,0:T(8,128)S(1)} %get-tuple-element.51), channel_id=1, source_target_pairs={{0,4},{1,5},{2,6},{3,7},{4,0},{5,1},{6,2},{7,3},{8,12},{9,13},{10,... | collective-permute-start | bytes 1572872 | tf_op jit(solution)/shard_map/ppermute | solution.py:329
  42.3 1.7 %collective-permute-start.10 = (f32[128,512]{1,0:T(8,128)S(1)}, f32[128,512]{1,0:T(8,128)S(1)}, u32[]{:S(2)}, u32[]{:S(2)}) collective-permute-start(f32[128,512]{1,0:T(8,128)S(1)} %get-tuple-element.45.refs_6_), channel_id=1, source_target_pairs={{0,1},{1,2},{2,3},{3,0},{4,5},{5,6},{6,7},{7,4},{8,9},{9,10},{10,1... | collective-permute-start | bytes 786440 | tf_op jit(solution)/shard_map/ppermute | solution.py:327
  44.0 1.5 %collective-permute-start.8 = (f32[128,512]{1,0:T(8,128)S(1)}, f32[128,512]{1,0:T(8,128)S(1)}, u32[]{:S(2)}, u32[]{:S(2)}) collective-permute-start(f32[128,512]{1,0:T(8,128)S(1)} %get-tuple-element.49), channel_id=1, source_target_pairs={{0,3},{1,0},{2,1},{3,2},{4,7},{5,4},{6,5},{7,6},{8,11},{9,8},{10,9... | collective-permute-start | bytes 786440 | tf_op jit(solution)/shard_map/ppermute | solution.py:328
  45.5 0.3 collective-permute-done.5.refs_5_
  46.0 0.5 collective-permute-start.7
  46.6 5.4 %collective-permute-done.10.refs_2_ = f32[128,512]{1,0:T(8,128)S(1)} collective-permute-done((f32[128,512]{1,0:T(8,128)S(1)}, f32[128,512]{1,0:T(8,128)S(1)}, u32[]{:S(2)}, u32[]{:S(2)}) %collective-permute-start.10) | collective-permute-done | bytes 262176 | tf_op jit(solution)/shard_map/ppermute | solution.py:327
  52.1 0.3 collective-permute-done.9.refs_4_
  52.5 3.6 %collective-permute-start.12 = (f32[256,512]{1,0:T(8,128)S(1)}, f32[256,512]{1,0:T(8,128)S(1)}, u32[]{:S(2)}, u32[]{:S(2)}) collective-permute-start(f32[256,512]{1,0:T(8,128)S(1)} %get-tuple-element.55), channel_id=1, source_target_pairs={{0,3},{1,0},{2,1},{3,2},{4,7},{5,4},{6,5},{7,6},{8,11},{9,8},{10,9... | collective-permute-start | bytes 1572872 | tf_op jit(solution)/shard_map/ppermute | solution.py:328
  56.1 7.5 %collective-permute-done.7.refs_1_ = f32[256,512]{1,0:T(8,128)S(1)} collective-permute-done((f32[256,512]{1,0:T(8,128)S(1)}, f32[256,512]{1,0:T(8,128)S(1)}, u32[]{:S(2)}, u32[]{:S(2)}) %collective-permute-start.7) | collective-permute-done | bytes 524320 | tf_op jit(solution)/shard_map/ppermute | solution.py:329
  63.6 0.9 shard_map.87
  64.5 0.5 collective-permute-done.11.refs_1_
  65.0 0.9 shard_map.88
  65.9 25.4 %all_to_all.10.value_ref = f32[32,8,128]{2,1,0:T(8,128)S(1)} all-to-all(f32[32,8,128]{2,1,0:T(8,128)S(1)} %get-tuple-element.60), channel_id=1, replica_groups={{0,16,32,48,64,80,96,112,8,24,40,56,72,88,104,120,128,144,160,176,192,2..., dimensions={0} | all-to-all | bytes 262144 | tf_op jit(solution)/shard_map/all_to_all | solution.py:377
  91.2 0.7 shard_map.89
  92.0 18.6 %all_to_all.11.refs_5_.mine_ref = f32[16,64,128]{2,1,0:T(8,128)S(1)} all-to-all(f32[16,64,128]{2,1,0:T(8,128)S(1)} %shard_map.89), channel_id=1, replica_groups={{0,16,32,48,64,80,96,112,128,144,160,176,192,208,224,240},{8,24,40,56,7..., dimensions={0} | all-to-all | bytes 1048576 | tf_op jit(solution)/shard_map/all_to_all | solution.py:380
  110.5 1.9 %collective-permute-start.13 = (f32[16,64,128]{2,1,0:T(8,128)S(1)}, f32[16,64,128]{2,1,0:T(8,128)S(1)}, u32[]{:S(2)}, u32[]{:S(2)}) collective-permute-start(f32[16,64,128]{2,1,0:T(8,128)S(1)} %all_to_all.11.refs_5_.mine_ref), channel_id=1, source_target_pairs={{0,8},{8,0},{16,24},{24,16},{32,40},{40,32},{48,56},{56,48},{64,72... | collective-permute-start | bytes 1572872 | tf_op jit(solution)/shard_map/ppermute | solution.py:330
  112.4 1.6 %shard_map.90 = f32[512,512]{1,0:T(8,128)} custom-call(f32[256,512]{1,0:T(8,128)S(1)} %get-tuple-element.54.refs_0_, f32[256,512]{1,0:T(8,128)S(1)} %get-tuple-element.57.refs_1_, f32[512,256]{1,0:T(8,128)S(1)} %get-tuple-element.58.refs_2_, f32[512,256]{1,0:T(8,128)S(1)} %get-tuple-element.59.refs_3_, bf16[384,128]{1,0:T(8,128)(2,1)S(1)} %copy-done.4, ...), custom_call_target="tpu_custom_call" | custom-call | flops 1 | bytes 1 | tf_op jit(solution)/shard_map/pallas_call | solution.py:254
  114.0 1.6 %shard_map.91 = f32[512,512]{1,0:T(8,128)} custom-call(f32[16,64,128]{2,1,0:T(8,128)S(1)} %all_to_all.11.refs_5_.mine_ref, f32[16,64,128]{2,1,0:T(8,128)S(1)} %collective-permute-done.13.other_ref, bf16[384,128]{1,0:T(8,128)(2,1)S(1)} %copy-done.4), custom_call_target="tpu_custom_call" | custom-call | flops 1 | bytes 1 | tf_op jit(solution)/shard_map/pallas_call | solution.py:307
  (23 shorter events, 0.6 us)
Async XLA Ops:
  4.9 35.2 %collective-permute-start.6 = (f32[768,512]{1,0:T(8,128)}, f32[768,512]{1,0:T(8,128)S(1)}, u32[]{:S(2)}, u32[]{:S(2)}) collective-permute-start(f32[768,512]{1,0:T(8,128)} %get-tuple-element.44), channel_id=1, source_target_pairs={{0,4},{1,5},{2,6},{3,7},{4,0},{5,1},{6,2},{7,3},{8,12},{9,13},{10,... | collective-permute-start | bytes 4718600 | tf_op jit(solution)/shard_map/ppermute | solution.py:329
  7.1 13.3 %collective-permute-start.1 = (f32[256,512]{1,0:T(8,128)}, f32[256,512]{1,0:T(8,128)S(1)}, u32[]{:S(2)}, u32[]{:S(2)}) collective-permute-start(f32[256,512]{1,0:T(8,128)} %get-tuple-element.36), channel_id=1, source_target_pairs={{0,3},{1,0},{2,1},{3,2},{4,7},{5,4},{6,5},{7,6},{8,11},{9,8},{10,9... | collective-permute-start | bytes 1572872 | tf_op jit(solution)/shard_map/ppermute | solution.py:328
  9.8 13.6 %collective-permute-start = (f32[256,512]{1,0:T(8,128)}, f32[256,512]{1,0:T(8,128)S(1)}, u32[]{:S(2)}, u32[]{:S(2)}) collective-permute-start(f32[256,512]{1,0:T(8,128)} %get-tuple-element.32.refs_0_), channel_id=1, source_target_pairs={{0,1},{1,2},{2,3},{3,0},{4,5},{5,6},{6,7},{7,4},{8,9},{9,10},{10,1... | collective-permute-start | bytes 1572872 | tf_op jit(solution)/shard_map/ppermute | solution.py:327
  12.6 29.7 %collective-permute-start.4 = (f32[256,512]{1,0:T(8,128)}, f32[256,512]{1,0:T(8,128)S(1)}, u32[]{:S(2)}, u32[]{:S(2)}) collective-permute-start(f32[256,512]{1,0:T(8,128)} %get-tuple-element.42), channel_id=1, source_target_pairs={{0,3},{1,0},{2,1},{3,2},{4,7},{5,4},{6,5},{7,6},{8,11},{9,8},{10,9... | collective-permute-start | bytes 1572872 | tf_op jit(solution)/shard_map/ppermute | solution.py:328
  15.3 28.6 %collective-permute-start.2 = (f32[256,512]{1,0:T(8,128)}, f32[256,512]{1,0:T(8,128)S(1)}, u32[]{:S(2)}, u32[]{:S(2)}) collective-permute-start(f32[256,512]{1,0:T(8,128)} %get-tuple-element.33.refs_0_), channel_id=1, source_target_pairs={{0,1},{1,2},{2,3},{3,0},{4,5},{5,6},{6,7},{7,4},{8,9},{9,10},{10,1... | collective-permute-start | bytes 1572872 | tf_op jit(solution)/shard_map/ppermute | solution.py:327
  15.3 1.1 copy-start.2
  18.4 6.6 %copy-start = (bf16[640,512]{1,0:T(8,128)(2,1)S(1)}, bf16[640,512]{1,0:T(8,128)(2,1)}, u32[]{:S(2)}) copy-start(bf16[640,512]{1,0:T(8,128)(2,1)} %cot_ref.7) | copy-start | bytes 1966084
  23.5 22.0 %collective-permute-start.3 = (f32[256,512]{1,0:T(8,128)S(1)}, f32[256,512]{1,0:T(8,128)S(1)}, u32[]{:S(2)}, u32[]{:S(2)}) collective-permute-start(f32[256,512]{1,0:T(8,128)S(1)} %get-tuple-element.40), channel_id=1, source_target_pairs={{0,3},{1,0},{2,1},{3,2},{4,7},{5,4},{6,5},{7,6},{8,11},{9,8},{10,9... | collective-permute-start | bytes 1572872 | tf_op jit(solution)/shard_map/ppermute | solution.py:328
  23.9 22.0 %collective-permute-start.5 = (f32[256,512]{1,0:T(8,128)S(1)}, f32[256,512]{1,0:T(8,128)S(1)}, u32[]{:S(2)}, u32[]{:S(2)}) collective-permute-start(f32[256,512]{1,0:T(8,128)S(1)} %get-tuple-element.38.refs_0_), channel_id=1, source_target_pairs={{0,1},{1,2},{2,3},{3,0},{4,5},{5,6},{6,7},{7,4},{8,9},{9,10},{10,1... | collective-permute-start | bytes 1572872 | tf_op jit(solution)/shard_map/ppermute | solution.py:327
  40.1 12.2 %collective-permute-start.9 = (f32[256,512]{1,0:T(8,128)S(1)}, f32[256,512]{1,0:T(8,128)S(1)}, u32[]{:S(2)}, u32[]{:S(2)}) collective-permute-start(f32[256,512]{1,0:T(8,128)S(1)} %get-tuple-element.51), channel_id=1, source_target_pairs={{0,4},{1,5},{2,6},{3,7},{4,0},{5,1},{6,2},{7,3},{8,12},{9,13},{10,... | collective-permute-start | bytes 1572872 | tf_op jit(solution)/shard_map/ppermute | solution.py:329
  42.3 9.6 %collective-permute-start.10 = (f32[128,512]{1,0:T(8,128)S(1)}, f32[128,512]{1,0:T(8,128)S(1)}, u32[]{:S(2)}, u32[]{:S(2)}) collective-permute-start(f32[128,512]{1,0:T(8,128)S(1)} %get-tuple-element.45.refs_6_), channel_id=1, source_target_pairs={{0,1},{1,2},{2,3},{3,0},{4,5},{5,6},{6,7},{7,4},{8,9},{9,10},{10,1... | collective-permute-start | bytes 786440 | tf_op jit(solution)/shard_map/ppermute | solution.py:327
  44.0 8.4 %collective-permute-start.8 = (f32[128,512]{1,0:T(8,128)S(1)}, f32[128,512]{1,0:T(8,128)S(1)}, u32[]{:S(2)}, u32[]{:S(2)}) collective-permute-start(f32[128,512]{1,0:T(8,128)S(1)} %get-tuple-element.49), channel_id=1, source_target_pairs={{0,3},{1,0},{2,1},{3,2},{4,7},{5,4},{6,5},{7,6},{8,11},{9,8},{10,9... | collective-permute-start | bytes 786440 | tf_op jit(solution)/shard_map/ppermute | solution.py:328
  46.0 17.6 %copy-start.1 = (f32[1,512,512]{2,1,0:T(8,128)S(1)}, f32[1,512,512]{2,1,0:T(8,128)}, u32[]{:S(2)}) copy-start(f32[1,512,512]{2,1,0:T(8,128)} %param.8) | copy-start | bytes 3145732
  46.0 17.6 %copy-start.3 = (bf16[128,384]{1,0:T(8,128)(2,1)S(1)}, bf16[128,384]{1,0:T(8,128)(2,1)}, u32[]{:S(2)}) copy-start(bf16[128,384]{1,0:T(8,128)(2,1)} %constant.4.clone.refs_4_.refs_5_) | copy-start | bytes 294916
  46.0 17.6 %collective-permute-start.7 = (f32[256,512]{1,0:T(8,128)S(1)}, f32[256,512]{1,0:T(8,128)S(1)}, u32[]{:S(2)}, u32[]{:S(2)}) collective-permute-start(f32[256,512]{1,0:T(8,128)S(1)} %get-tuple-element.47.refs_3_), channel_id=1, source_target_pairs={{0,4},{1,5},{2,6},{3,7},{4,0},{5,1},{6,2},{7,3},{8,12},{9,13},{10,... | collective-permute-start | bytes 1572872 | tf_op jit(solution)/shard_map/ppermute | solution.py:329
  52.0 13.0 %collective-permute-start.11 = (f32[256,512]{1,0:T(8,128)S(1)}, f32[256,512]{1,0:T(8,128)S(1)}, u32[]{:S(2)}, u32[]{:S(2)}) collective-permute-start(f32[256,512]{1,0:T(8,128)S(1)} %shard_map.85.refs_5_), channel_id=1, source_target_pairs={{0,1},{1,2},{2,3},{3,0},{4,5},{5,6},{6,7},{7,4},{8,9},{9,10},{10,1... | collective-permute-start | bytes 1572872 | tf_op jit(solution)/shard_map/ppermute | solution.py:327
  52.5 60.0 %copy-start.4 = (bf16[384,128]{1,0:T(8,128)(2,1)S(1)}, bf16[384,128]{1,0:T(8,128)(2,1)}, u32[]{:S(2)}) copy-start(bf16[384,128]{1,0:T(8,128)(2,1)} %constant.5.clone.refs_4_.cos_ref) | copy-start | bytes 294916
  52.5 12.5 %collective-permute-start.12 = (f32[256,512]{1,0:T(8,128)S(1)}, f32[256,512]{1,0:T(8,128)S(1)}, u32[]{:S(2)}, u32[]{:S(2)}) collective-permute-start(f32[256,512]{1,0:T(8,128)S(1)} %get-tuple-element.55), channel_id=1, source_target_pairs={{0,3},{1,0},{2,1},{3,2},{4,7},{5,4},{6,5},{7,6},{8,11},{9,8},{10,9... | collective-permute-start | bytes 1572872 | tf_op jit(solution)/shard_map/ppermute | solution.py:328
  110.5 3.5 %collective-permute-start.13 = (f32[16,64,128]{2,1,0:T(8,128)S(1)}, f32[16,64,128]{2,1,0:T(8,128)S(1)}, u32[]{:S(2)}, u32[]{:S(2)}) collective-permute-start(f32[16,64,128]{2,1,0:T(8,128)S(1)} %all_to_all.11.refs_5_.mine_ref), channel_id=1, source_target_pairs={{0,8},{8,0},{16,24},{24,16},{32,40},{40,32},{48,56},{56,48},{64,72... | collective-permute-start | bytes 1572872 | tf_op jit(solution)/shard_map/ppermute | solution.py:330

commit v4 on v3

--- a/solution.py
+++ b/solution.py
@@ -213,7 +213,7 @@
                     taken = jnp.where(hit, own, 0.0)
                     kept = jnp.sum(taken, axis=0, keepdims=True)
                     for p in range(HALF // PART):
-                        at = (len(before) * HALF // PART + p) * 2 * pairs + c
+                        at = (len(before) * 2 * pairs + c) * (HALF // PART) + p
                         kept_ref[at, j : j + 1, :] = kept[:, p * PART : (p + 1) * PART]
                     filled = filled + taken
                 masked_ref[c * BLOCK : (c + 1) * BLOCK, :] = filled
@@ -269,10 +269,9 @@
         frequency = lax.broadcasted_iota(jnp.int32, (BLOCK, rows), 0).astype(F32)
 
         def add(m, total):
-            replica = m // (NC * NZ) * (NC * NZ) + m % NZ * NC + m // NZ % NC
             own = jnp.zeros((BLOCK, rows), F32)
             for j in range(keep):
-                hit = frequency == chosen_ref[replica, j : j + 1, :]
+                hit = frequency == chosen_ref[m, j : j + 1, :]
                 own = jnp.where(hit, value_ref[m, j : j + 1, :], own)
             return total + own
 
@@ -355,26 +354,23 @@
         [[(HALF, [(other, 0), (a2, 0), (b3, 0)])], [(HALF, [(own, 0), (b2, 0), (a3, 0)])]], after=[q2a]
     )
     received = to_across(other)
+    (q3a,) = combine([[(PART, [(q3, 0), (rx21, 2 * HALF)])]], after=[other])
+    qba = to_down(q3a)
     (q1,) = combine(
-        [[(PART, [(q1, 0), (rx21, HALF), (qa1, 0)]), (PART, [(q1, PART), (rx21, HALF + PART)])]], after=[other]
+        [[(PART, [(q1, 0), (rx21, HALF), (qa1, 0)]), (PART, [(q1, PART), (rx21, HALF + PART)])]], after=[q3a]
     )
     qa = to_up(q1)
-    q3, q0 = combine(
-        [
-            [(PART, [(q3, 0), (rx21, 2 * HALF)]), (PART, [(q3, PART), (rx21, 2 * HALF + PART), (qb1, 0)])],
-            [(HALF, [(q0, 0), (rx0, 0)])],
-        ],
-        after=[q1],
-    )
-    qb = to_down(q3)
+    q3b, q0 = combine(
+        [[(PART, [(q3, PART), (rx21, 2 * HALF + PART), (qb1, 0)])], [(HALF, [(q0, 0), (rx0, 0)])]], after=[q1]
+    )
+    qbb = to_down(q3b)
 
     pieces0 = [(piece, 0, 0, HALF) for piece in (own, received)]
-    pieces1 = [(piece, 0, 0, HALF) for piece in (q0, qa, qb)]
+    pieces1 = [(q0, 0, 0, HALF), (qa, 0, 0, HALF), (qba, 0, 0, PART), (qbb, 0, PART, PART)]
     kept, moment0, masked0 = select(pieces0, momentum[0], 0, factor, own_chosen, forward_cos, None, after=[q0])
     kept, moment1, masked1 = select(pieces1, momentum[0], 1, factor, own_chosen, forward_cos, kept)
 
-    order = [i * NZ * NC + j * NC + k for i in range(NH) for k in range(NC) for j in range(NZ)]
-    kept = lax.all_to_all(kept, "replica", 0, 0, tiled=True, axis_index_groups=[order])
+    kept = lax.all_to_all(kept, "replica", 0, 0, tiled=True)
     summed = spread(kept, all_chosen, NH * NZ)
     cores = [[i * NZ * NC + j * NC + k for i in range(NH) for j in range(NZ)] for k in range(NC)]
     mine = lax.all_to_all(summed, "replica", 0, 0, tiled=True, axis_index_groups=cores)

time: 116 us -> 114 us (0.983)
  blocking collectives: 43.9 us -> 40.6 us
  waiting for transfers between devices: 28.3 us -> 29.9 us
    all_to_all x1, blocking collectives: 18.6 us -> 16.8 us  [on_device(): lax.all_to_all(summed, 'replica', 0, 0, tiled=True, axis_index_groups=cores)]
    ppermute x1, starting transfers between devices: 1.88 us -> 3.45 us  [on_device(): lax.ppermute(v, 'replica', [(i, i ^ 1) for i in range(replicas)])]
    all_to_all x1, blocking collectives: 25.4 us -> 23.8 us  [on_device(): kept = lax.all_to_all(kept, 'replica', 0, 0, tiled=True)]
    ppermute x5 -> x6, starting transfers between devices: 11 us -> 10.1 us  [on_device(): to_down = lambda v: lax.ppermute(v, 'fsdp', down)]
  transfers between devices with their start and end apart: 14 -> 15, of which waited for: 8 -> 7; matrix products, arithmetic and copies ran while one was open for 0% -> 0% of each run, Pallas kernels for 12% -> 12%
where the time goes in v4:
time: 114 us
  blocking collectives  40.6 us (36%)
  waiting for transfers between devices  29.9 us (26%)
  starting transfers between devices  21 us (18%)
  Pallas kernels  20.8 us (18%)
    all_to_all x1, blocking collectives, on_device(): kept = lax.all_to_all(kept, 'replica', 0, 0, tiled=True)  23.8 us
    ppermute x3, waiting for transfers between devices, on_device(): to_across = lambda v: lax.ppermute(v, 'fsdp', across)  18.6 us
    all_to_all x1, blocking collectives, on_device(): lax.all_to_all(summed, 'replica', 0, 0, tiled=True, axis_index_groups=cores)  16.8 us
    pallas_call x4, Pallas kernels, products(): pl.pallas_call(kernel, out_shape=[jax.ShapeDtypeStruct(s, F32) for s in s...  13 us
    ppermute x6, starting transfers between devices, on_device(): to_down = lambda v: lax.ppermute(v, 'fsdp', down)  10.1 us
    ppermute x5, waiting for transfers between devices, on_device(): to_up = lambda v: lax.ppermute(v, 'fsdp', up)  10.1 us
    ppermute x3, starting transfers between devices, on_device(): to_across = lambda v: lax.ppermute(v, 'fsdp', across)  4.57 us
    ppermute x1, starting transfers between devices, on_device(): lax.ppermute(v, 'replica', [(i, i ^ 1) for i in range(replicas)])  3.45 us
  transfers between devices with their start and end apart: 15, of which 7 were waited for; matrix products, arithmetic and copies ran while one was open for 0% of the time, Pallas kernels for 12%

profile of v4, /device:TPU:1, one launch (start us, length us, event | category | flops | bytes accessed | tf_op | source)
XLA Modules:
  0.0 114.2 jit_solution(12066223587512520306)
XLA Ops:
  0.6 4.3 %shard_map.77 = (f32[768,512]{1,0:T(8,128)}, f32[256,512]{1,0:T(8,128)}, f32[256,512]{1,0:T(8,128)}) custom-call(bf16[640,4096]{1,0:T(8,128)(2,1)} %tokens_ref.7, bf16[640,512]{1,0:T(8,128)(2,1)} %cot_ref.7), custom_call_target="tpu_custom_call" | custom-call | flops 1 | bytes 1 | tf_op jit(solution)/shard_map/pallas_call | solution.py:76
  4.9 2.1 %collective-permute-start.6 = (f32[768,512]{1,0:T(8,128)}, f32[768,512]{1,0:T(8,128)S(1)}, u32[]{:S(2)}, u32[]{:S(2)}) collective-permute-start(f32[768,512]{1,0:T(8,128)} %get-tuple-element.44), channel_id=1, source_target_pairs={{0,4},{1,5},{2,6},{3,7},{4,0},{5,1},{6,2},{7,3},{8,12},{9,13},{10,... | collective-permute-start | bytes 4718600 | tf_op jit(solution)/shard_map/ppermute | solution.py:328
  7.1 2.7 %collective-permute-start.1 = (f32[256,512]{1,0:T(8,128)}, f32[256,512]{1,0:T(8,128)S(1)}, u32[]{:S(2)}, u32[]{:S(2)}) collective-permute-start(f32[256,512]{1,0:T(8,128)} %get-tuple-element.36), channel_id=1, source_target_pairs={{0,3},{1,0},{2,1},{3,2},{4,7},{5,4},{6,5},{7,6},{8,11},{9,8},{10,9... | collective-permute-start | bytes 1572872 | tf_op jit(solution)/shard_map/ppermute | solution.py:327
  9.8 2.8 %shard_map.78 = (f32[256,512]{1,0:T(8,128)}, f32[256,512]{1,0:T(8,128)}) custom-call(bf16[640,4096]{1,0:T(8,128)(2,1)} %tokens_ref.7, bf16[640,512]{1,0:T(8,128)(2,1)} %cot_ref.7, f32[256,512]{1,0:T(8,128)} %get-tuple-element.32.refs_0_), custom_call_target="tpu_custom_call" | custom-call | flops 1 | bytes 1 | tf_op jit(solution)/shard_map/pallas_call | solution.py:76
  12.6 2.8 %collective-permute-start.4 = (f32[256,512]{1,0:T(8,128)}, f32[256,512]{1,0:T(8,128)S(1)}, u32[]{:S(2)}, u32[]{:S(2)}) collective-permute-start(f32[256,512]{1,0:T(8,128)} %get-tuple-element.42), channel_id=1, source_target_pairs={{0,3},{1,0},{2,1},{3,2},{4,7},{5,4},{6,5},{7,6},{8,11},{9,8},{10,9... | collective-permute-start | bytes 1572872 | tf_op jit(solution)/shard_map/ppermute | solution.py:327
  15.3 1.1 copy-done.2
  16.4 2.0 %shard_map.79 = (f32[256,512]{1,0:T(8,128)S(1)}, f32[256,512]{1,0:T(8,128)S(1)}) custom-call(bf16[640,4096]{1,0:T(8,128)(2,1)} %tokens_ref.7, bf16[640,512]{1,0:T(8,128)(2,1)} %cot_ref.7, f32[256,512]{1,0:T(8,128)S(1)} %copy-done.2), custom_call_target="tpu_custom_call" | custom-call | flops 1 | bytes 1 | tf_op jit(solution)/shard_map/pallas_call | solution.py:76
  18.4 1.7 %shard_map.80 = (f32[8,8,512]{2,1,0:T(8,128)S(1)}, f32[32,8,128]{2,1,0:T(8,128)S(1)}) custom-call(s32[32,8,4096]{2,1,0:T(8,128)} %index_ref.1, f32[256,512]{1,0:T(8,128)S(1)} %get-tuple-element.34.refs_0_), custom_call_target="tpu_custom_call" | custom-call | flops 1 | bytes 1 | tf_op jit(solution)/shard_map/pallas_call | solution.py:160
  20.1 0.3 collective-permute-done.1.refs_3_
  20.4 3.0 %collective-permute-done.refs_1_ = f32[256,512]{1,0:T(8,128)S(1)} collective-permute-done((f32[256,512]{1,0:T(8,128)}, f32[256,512]{1,0:T(8,128)S(1)}, u32[]{:S(2)}, u32[]{:S(2)}) %collective-permute-start) | collective-permute-done | bytes 524320 | tf_op jit(solution)/shard_map/ppermute | solution.py:326
  23.5 0.4 collective-permute-start.3
  23.9 1.2 %collective-permute-start.5 = (f32[256,512]{1,0:T(8,128)S(1)}, f32[256,512]{1,0:T(8,128)S(1)}, u32[]{:S(2)}, u32[]{:S(2)}) collective-permute-start(f32[256,512]{1,0:T(8,128)S(1)} %get-tuple-element.38.refs_0_), channel_id=1, source_target_pairs={{0,1},{1,2},{2,3},{3,0},{4,5},{5,6},{6,7},{7,4},{8,9},{9,10},{10,1... | collective-permute-start | bytes 1572872 | tf_op jit(solution)/shard_map/ppermute | solution.py:326
  25.0 4.0 %shard_map.82 = (f32[256,512]{1,0:T(8,128)S(1)}, f32[256,512]{1,0:T(8,128)S(1)}, f32[256,512]{1,0:T(8,128)S(1)}, f32[256,512]{1,0:T(8,128)S(1)}, f32[256,512]{1,...) custom-call(bf16[640,4096]{1,0:T(8,128)(2,1)} %tokens_ref.7, bf16[640,512]{1,0:T(8,128)(2,1)S(1)} %copy-done, ...), custom_call_target="tpu_custom_call" | custom-call | flops 1 | bytes 1 | tf_op jit(solution)/shard_map/pallas_call | solution.py:76
  29.0 11.1 %collective-permute-done.6.refs_1_ = f32[768,512]{1,0:T(8,128)S(1)} collective-permute-done((f32[768,512]{1,0:T(8,128)}, f32[768,512]{1,0:T(8,128)S(1)}, u32[]{:S(2)}, u32[]{:S(2)}) %collective-permute-start.6) | collective-permute-done | bytes 1572896 | tf_op jit(solution)/shard_map/ppermute | solution.py:328
  40.1 2.1 %collective-permute-start.9 = (f32[256,512]{1,0:T(8,128)S(1)}, f32[256,512]{1,0:T(8,128)S(1)}, u32[]{:S(2)}, u32[]{:S(2)}) collective-permute-start(f32[256,512]{1,0:T(8,128)S(1)} %get-tuple-element.51), channel_id=1, source_target_pairs={{0,4},{1,5},{2,6},{3,7},{4,0},{5,1},{6,2},{7,3},{8,12},{9,13},{10,... | collective-permute-start | bytes 1572872 | tf_op jit(solution)/shard_map/ppermute | solution.py:328
  42.3 1.7 %collective-permute-start.10 = (f32[128,512]{1,0:T(8,128)S(1)}, f32[128,512]{1,0:T(8,128)S(1)}, u32[]{:S(2)}, u32[]{:S(2)}) collective-permute-start(f32[128,512]{1,0:T(8,128)S(1)} %get-tuple-element.45.refs_6_), channel_id=1, source_target_pairs={{0,1},{1,2},{2,3},{3,0},{4,5},{5,6},{6,7},{7,4},{8,9},{9,10},{10,1... | collective-permute-start | bytes 786440 | tf_op jit(solution)/shard_map/ppermute | solution.py:326
  44.0 1.9 %collective-permute-done.5.refs_5_ = f32[256,512]{1,0:T(8,128)S(1)} collective-permute-done((f32[256,512]{1,0:T(8,128)S(1)}, f32[256,512]{1,0:T(8,128)S(1)}, u32[]{:S(2)}, u32[]{:S(2)}) %collective-permute-start.5) | collective-permute-done | bytes 524320 | tf_op jit(solution)/shard_map/ppermute | solution.py:326
  46.0 0.3 collective-permute-start.7
  46.4 0.3 collective-permute-start.8
  46.7 5.2 %collective-permute-done.10.refs_2_ = f32[128,512]{1,0:T(8,128)S(1)} collective-permute-done((f32[128,512]{1,0:T(8,128)S(1)}, f32[128,512]{1,0:T(8,128)S(1)}, u32[]{:S(2)}, u32[]{:S(2)}) %collective-permute-start.10) | collective-permute-done | bytes 262176 | tf_op jit(solution)/shard_map/ppermute | solution.py:326
  52.1 2.7 %collective-permute-start.12 = (f32[128,512]{1,0:T(8,128)S(1)}, f32[128,512]{1,0:T(8,128)S(1)}, u32[]{:S(2)}, u32[]{:S(2)}) collective-permute-start(f32[128,512]{1,0:T(8,128)S(1)} %shard_map.85.refs_3_), channel_id=1, source_target_pairs={{0,3},{1,0},{2,1},{3,2},{4,7},{5,4},{6,5},{7,6},{8,11},{9,8},{10,9... | collective-permute-start | bytes 786440 | tf_op jit(solution)/shard_map/ppermute | solution.py:327
  54.9 1.3 %collective-permute-start.13 = (f32[128,512]{1,0:T(8,128)S(1)}, f32[128,512]{1,0:T(8,128)S(1)}, u32[]{:S(2)}, u32[]{:S(2)}) collective-permute-start(f32[128,512]{1,0:T(8,128)S(1)} %get-tuple-element.55), channel_id=1, source_target_pairs={{0,3},{1,0},{2,1},{3,2},{4,7},{5,4},{6,5},{7,6},{8,11},{9,8},{10,9... | collective-permute-start | bytes 786440 | tf_op jit(solution)/shard_map/ppermute | solution.py:327
  56.1 7.5 %collective-permute-done.7.refs_1_ = f32[256,512]{1,0:T(8,128)S(1)} collective-permute-done((f32[256,512]{1,0:T(8,128)S(1)}, f32[256,512]{1,0:T(8,128)S(1)}, u32[]{:S(2)}, u32[]{:S(2)}) %collective-permute-start.7) | collective-permute-done | bytes 524320 | tf_op jit(solution)/shard_map/ppermute | solution.py:328
  63.6 0.9 shard_map.88
  64.5 1.0 collective-permute-done.13.refs_3_
  65.5 0.9 shard_map.89
  66.4 23.8 %all_to_all.10.value_ref = f32[32,8,128]{2,1,0:T(8,128)S(1)} all-to-all(f32[32,8,128]{2,1,0:T(8,128)S(1)} %get-tuple-element.60), channel_id=1, replica_groups=mesh['replica'=32,'fsdp'=8] {'replica'}, dimensions={0} | all-to-all | bytes 262144 | tf_op jit(solution)/shard_map/all_to_all | solution.py:373
  90.2 0.6 shard_map.90
  90.8 16.8 %all_to_all.11.refs_5_.mine_ref = f32[16,64,128]{2,1,0:T(8,128)S(1)} all-to-all(f32[16,64,128]{2,1,0:T(8,128)S(1)} %shard_map.90), channel_id=1, replica_groups={{0,16,32,48,64,80,96,112,128,144,160,176,192,208,224,240},{8,24,40,56,7..., dimensions={0} | all-to-all | bytes 1048576 | tf_op jit(solution)/shard_map/all_to_all | solution.py:376
  107.6 3.5 %collective-permute-start.14 = (f32[16,64,128]{2,1,0:T(8,128)S(1)}, f32[16,64,128]{2,1,0:T(8,128)S(1)}, u32[]{:S(2)}, u32[]{:S(2)}) collective-permute-start(f32[16,64,128]{2,1,0:T(8,128)S(1)} %all_to_all.11.refs_5_.mine_ref), channel_id=1, source_target_pairs={{0,8},{8,0},{16,24},{24,16},{32,40},{40,32},{48,56},{56,48},{64,72... | collective-permute-start | bytes 1572872 | tf_op jit(solution)/shard_map/ppermute | solution.py:329
  111.0 1.6 %shard_map.91 = f32[512,512]{1,0:T(8,128)} custom-call(f32[256,512]{1,0:T(8,128)S(1)} %get-tuple-element.54.refs_0_, f32[256,512]{1,0:T(8,128)S(1)} %get-tuple-element.57.refs_1_, f32[512,256]{1,0:T(8,128)S(1)} %get-tuple-element.58.refs_2_, f32[512,256]{1,0:T(8,128)S(1)} %get-tuple-element.59.refs_3_, bf16[384,128]{1,0:T(8,128)(2,1)S(1)} %copy-done.4, ...), custom_call_target="tpu_custom_call" | custom-call | flops 1 | bytes 1 | tf_op jit(solution)/shard_map/pallas_call | solution.py:254
  112.6 1.6 %shard_map.92 = f32[512,512]{1,0:T(8,128)} custom-call(f32[16,64,128]{2,1,0:T(8,128)S(1)} %all_to_all.11.refs_5_.mine_ref, f32[16,64,128]{2,1,0:T(8,128)S(1)} %collective-permute-done.14.other_ref, bf16[384,128]{1,0:T(8,128)(2,1)S(1)} %copy-done.4), custom_call_target="tpu_custom_call" | custom-call | flops 1 | bytes 1 | tf_op jit(solution)/shard_map/pallas_call | solution.py:306
  (26 shorter events, 0.6 us)
Async XLA Ops:
  4.9 35.2 %collective-permute-start.6 = (f32[768,512]{1,0:T(8,128)}, f32[768,512]{1,0:T(8,128)S(1)}, u32[]{:S(2)}, u32[]{:S(2)}) collective-permute-start(f32[768,512]{1,0:T(8,128)} %get-tuple-element.44), channel_id=1, source_target_pairs={{0,4},{1,5},{2,6},{3,7},{4,0},{5,1},{6,2},{7,3},{8,12},{9,13},{10,... | collective-permute-start | bytes 4718600 | tf_op jit(solution)/shard_map/ppermute | solution.py:328
  7.1 13.3 %collective-permute-start.1 = (f32[256,512]{1,0:T(8,128)}, f32[256,512]{1,0:T(8,128)S(1)}, u32[]{:S(2)}, u32[]{:S(2)}) collective-permute-start(f32[256,512]{1,0:T(8,128)} %get-tuple-element.36), channel_id=1, source_target_pairs={{0,3},{1,0},{2,1},{3,2},{4,7},{5,4},{6,5},{7,6},{8,11},{9,8},{10,9... | collective-permute-start | bytes 1572872 | tf_op jit(solution)/shard_map/ppermute | solution.py:327
  9.8 13.6 %collective-permute-start = (f32[256,512]{1,0:T(8,128)}, f32[256,512]{1,0:T(8,128)S(1)}, u32[]{:S(2)}, u32[]{:S(2)}) collective-permute-start(f32[256,512]{1,0:T(8,128)} %get-tuple-element.32.refs_0_), channel_id=1, source_target_pairs={{0,1},{1,2},{2,3},{3,0},{4,5},{5,6},{6,7},{7,4},{8,9},{9,10},{10,1... | collective-permute-start | bytes 1572872 | tf_op jit(solution)/shard_map/ppermute | solution.py:326
  12.6 29.7 %collective-permute-start.4 = (f32[256,512]{1,0:T(8,128)}, f32[256,512]{1,0:T(8,128)S(1)}, u32[]{:S(2)}, u32[]{:S(2)}) collective-permute-start(f32[256,512]{1,0:T(8,128)} %get-tuple-element.42), channel_id=1, source_target_pairs={{0,3},{1,0},{2,1},{3,2},{4,7},{5,4},{6,5},{7,6},{8,11},{9,8},{10,9... | collective-permute-start | bytes 1572872 | tf_op jit(solution)/shard_map/ppermute | solution.py:327
  15.3 28.6 %collective-permute-start.2 = (f32[256,512]{1,0:T(8,128)}, f32[256,512]{1,0:T(8,128)S(1)}, u32[]{:S(2)}, u32[]{:S(2)}) collective-permute-start(f32[256,512]{1,0:T(8,128)} %get-tuple-element.33.refs_0_), channel_id=1, source_target_pairs={{0,1},{1,2},{2,3},{3,0},{4,5},{5,6},{6,7},{7,4},{8,9},{9,10},{10,1... | collective-permute-start | bytes 1572872 | tf_op jit(solution)/shard_map/ppermute | solution.py:326
  15.3 1.1 copy-start.2
  18.4 6.6 %copy-start = (bf16[640,512]{1,0:T(8,128)(2,1)S(1)}, bf16[640,512]{1,0:T(8,128)(2,1)}, u32[]{:S(2)}) copy-start(bf16[640,512]{1,0:T(8,128)(2,1)} %cot_ref.7) | copy-start | bytes 1966084
  23.5 20.5 %collective-permute-start.3 = (f32[256,512]{1,0:T(8,128)S(1)}, f32[256,512]{1,0:T(8,128)S(1)}, u32[]{:S(2)}, u32[]{:S(2)}) collective-permute-start(f32[256,512]{1,0:T(8,128)S(1)} %get-tuple-element.40), channel_id=1, source_target_pairs={{0,3},{1,0},{2,1},{3,2},{4,7},{5,4},{6,5},{7,6},{8,11},{9,8},{10,9... | collective-permute-start | bytes 1572872 | tf_op jit(solution)/shard_map/ppermute | solution.py:327
  23.9 22.0 %collective-permute-start.5 = (f32[256,512]{1,0:T(8,128)S(1)}, f32[256,512]{1,0:T(8,128)S(1)}, u32[]{:S(2)}, u32[]{:S(2)}) collective-permute-start(f32[256,512]{1,0:T(8,128)S(1)} %get-tuple-element.38.refs_0_), channel_id=1, source_target_pairs={{0,1},{1,2},{2,3},{3,0},{4,5},{5,6},{6,7},{7,4},{8,9},{9,10},{10,1... | collective-permute-start | bytes 1572872 | tf_op jit(solution)/shard_map/ppermute | solution.py:326
  40.1 14.6 %collective-permute-start.9 = (f32[256,512]{1,0:T(8,128)S(1)}, f32[256,512]{1,0:T(8,128)S(1)}, u32[]{:S(2)}, u32[]{:S(2)}) collective-permute-start(f32[256,512]{1,0:T(8,128)S(1)} %get-tuple-element.51), channel_id=1, source_target_pairs={{0,4},{1,5},{2,6},{3,7},{4,0},{5,1},{6,2},{7,3},{8,12},{9,13},{10,... | collective-permute-start | bytes 1572872 | tf_op jit(solution)/shard_map/ppermute | solution.py:328
  42.3 9.6 %collective-permute-start.10 = (f32[128,512]{1,0:T(8,128)S(1)}, f32[128,512]{1,0:T(8,128)S(1)}, u32[]{:S(2)}, u32[]{:S(2)}) collective-permute-start(f32[128,512]{1,0:T(8,128)S(1)} %get-tuple-element.45.refs_6_), channel_id=1, source_target_pairs={{0,1},{1,2},{2,3},{3,0},{4,5},{5,6},{6,7},{7,4},{8,9},{9,10},{10,1... | collective-permute-start | bytes 786440 | tf_op jit(solution)/shard_map/ppermute | solution.py:326
  46.0 17.6 %collective-permute-start.7 = (f32[256,512]{1,0:T(8,128)S(1)}, f32[256,512]{1,0:T(8,128)S(1)}, u32[]{:S(2)}, u32[]{:S(2)}) collective-permute-start(f32[256,512]{1,0:T(8,128)S(1)} %get-tuple-element.47.refs_2_), channel_id=1, source_target_pairs={{0,4},{1,5},{2,6},{3,7},{4,0},{5,1},{6,2},{7,3},{8,12},{9,13},{10,... | collective-permute-start | bytes 1572872 | tf_op jit(solution)/shard_map/ppermute | solution.py:328
  46.4 8.4 %collective-permute-start.8 = (f32[128,512]{1,0:T(8,128)S(1)}, f32[128,512]{1,0:T(8,128)S(1)}, u32[]{:S(2)}, u32[]{:S(2)}) collective-permute-start(f32[128,512]{1,0:T(8,128)S(1)} %get-tuple-element.49), channel_id=1, source_target_pairs={{0,3},{1,0},{2,1},{3,2},{4,7},{5,4},{6,5},{7,6},{8,11},{9,8},{10,9... | collective-permute-start | bytes 786440 | tf_op jit(solution)/shard_map/ppermute | solution.py:327
  46.7 16.9 %copy-start.1 = (f32[1,512,512]{2,1,0:T(8,128)S(1)}, f32[1,512,512]{2,1,0:T(8,128)}, u32[]{:S(2)}) copy-start(f32[1,512,512]{2,1,0:T(8,128)} %param.8) | copy-start | bytes 3145732
  46.7 16.9 %copy-start.3 = (bf16[128,384]{1,0:T(8,128)(2,1)S(1)}, bf16[128,384]{1,0:T(8,128)(2,1)}, u32[]{:S(2)}) copy-start(bf16[128,384]{1,0:T(8,128)(2,1)} %constant.4.clone.refs_4_.refs_6_) | copy-start | bytes 294916
  52.0 13.5 %collective-permute-start.11 = (f32[256,512]{1,0:T(8,128)S(1)}, f32[256,512]{1,0:T(8,128)S(1)}, u32[]{:S(2)}, u32[]{:S(2)}) collective-permute-start(f32[256,512]{1,0:T(8,128)S(1)} %shard_map.86.refs_5_), channel_id=1, source_target_pairs={{0,1},{1,2},{2,3},{3,0},{4,5},{5,6},{6,7},{7,4},{8,9},{9,10},{10,1... | collective-permute-start | bytes 1572872 | tf_op jit(solution)/shard_map/ppermute | solution.py:326
  52.1 12.4 %collective-permute-start.12 = (f32[128,512]{1,0:T(8,128)S(1)}, f32[128,512]{1,0:T(8,128)S(1)}, u32[]{:S(2)}, u32[]{:S(2)}) collective-permute-start(f32[128,512]{1,0:T(8,128)S(1)} %shard_map.85.refs_3_), channel_id=1, source_target_pairs={{0,3},{1,0},{2,1},{3,2},{4,7},{5,4},{6,5},{7,6},{8,11},{9,8},{10,9... | collective-permute-start | bytes 786440 | tf_op jit(solution)/shard_map/ppermute | solution.py:327
  54.8 56.2 %copy-start.4 = (bf16[384,128]{1,0:T(8,128)(2,1)S(1)}, bf16[384,128]{1,0:T(8,128)(2,1)}, u32[]{:S(2)}) copy-start(bf16[384,128]{1,0:T(8,128)(2,1)} %constant.5.clone.refs_4_.cos_ref) | copy-start | bytes 294916
  54.9 10.6 %collective-permute-start.13 = (f32[128,512]{1,0:T(8,128)S(1)}, f32[128,512]{1,0:T(8,128)S(1)}, u32[]{:S(2)}, u32[]{:S(2)}) collective-permute-start(f32[128,512]{1,0:T(8,128)S(1)} %get-tuple-element.55), channel_id=1, source_target_pairs={{0,3},{1,0},{2,1},{3,2},{4,7},{5,4},{6,5},{7,6},{8,11},{9,8},{10,9... | collective-permute-start | bytes 786440 | tf_op jit(solution)/shard_map/ppermute | solution.py:327
  107.6 5.0 %collective-permute-start.14 = (f32[16,64,128]{2,1,0:T(8,128)S(1)}, f32[16,64,128]{2,1,0:T(8,128)S(1)}, u32[]{:S(2)}, u32[]{:S(2)}) collective-permute-start(f32[16,64,128]{2,1,0:T(8,128)S(1)} %all_to_all.11.refs_5_.mine_ref), channel_id=1, source_target_pairs={{0,8},{8,0},{16,24},{24,16},{32,40},{40,32},{48,56},{56,48},{64,72... | collective-permute-start | bytes 1572872 | tf_op jit(solution)/shard_map/ppermute | solution.py:329

commit v5 on v4

--- a/solution.py
+++ b/solution.py
@@ -292,22 +292,29 @@
 def finish(mine, other, inverse_cos, scale):
     width = mine.shape[0] // NH * BLOCK
 
-    def kernel(mine_ref, other_ref, cos_ref, out_ref):
+    def kernel(mine_ref, other_ref, cos_ref, out_ref, made, sems):
         core = lax.axis_index("replica") % NC
         cos = cos_ref[...]
+        copies = []
         for ref, place in ((mine_ref, core), (other_ref, 1 - core)):
             for h in range(NH):
-                first = pl.multiple_of((h * NC + place) * PART, PART)
+                part = len(copies)
                 for g in range(width // PART):
                     at = h * (width // BLOCK) + 2 * g
                     spectra = jnp.concatenate([ref[at], ref[at + 1]], axis=0)
-                    out_ref[pl.ds(first, PART), PART * g : PART * (g + 1)] = scale * inverse_of(spectra, cos)
+                    made[part, :, PART * g : PART * (g + 1)] = scale * inverse_of(spectra, cos)
+                first = pl.multiple_of((h * NC + place) * PART, PART)
+                copies.append(pltpu.make_async_copy(made.at[part], out_ref.at[pl.ds(first, PART), :], sems.at[part]))
+                copies[-1].start()
+        for copy in copies:
+            copy.wait()
 
     return pl.pallas_call(
         kernel,
         out_shape=jax.ShapeDtypeStruct((NH * NC * PART, width), F32),
         in_specs=[VMEM] * 3,
-        out_specs=VMEM,
+        out_specs=ANY,
+        scratch_shapes=[pltpu.VMEM((NH * NC, PART, width), F32), pltpu.SemaphoreType.DMA((NH * NC,))],
         compiler_params=pltpu.CompilerParams(vmem_limit_bytes=24 << 20),
         cost_estimate=COST,
     )(mine, other, inverse_cos)

time: 114 us -> 114 us (level)
  no operation moved by 1% of the time
where the time goes in v5:
time: 114 us
  blocking collectives  40.6 us (36%)
  waiting for transfers between devices  29.9 us (26%)
  starting transfers between devices  21 us (18%)
  Pallas kernels  20.6 us (18%)
    all_to_all x1, blocking collectives, on_device(): kept = lax.all_to_all(kept, 'replica', 0, 0, tiled=True)  23.8 us
    ppermute x3, waiting for transfers between devices, on_device(): to_across = lambda v: lax.ppermute(v, 'fsdp', across)  18.6 us
    all_to_all x1, blocking collectives, on_device(): lax.all_to_all(summed, 'replica', 0, 0, tiled=True, axis_index_groups=cores)  16.8 us
    pallas_call x4, Pallas kernels, products(): pl.pallas_call(kernel, out_shape=[jax.ShapeDtypeStruct(s, F32) for s in s...  13 us
    ppermute x6, starting transfers between devices, on_device(): to_down = lambda v: lax.ppermute(v, 'fsdp', down)  10.1 us
    ppermute x5, waiting for transfers between devices, on_device(): to_up = lambda v: lax.ppermute(v, 'fsdp', up)  10.1 us
    ppermute x3, starting transfers between devices, on_device(): to_across = lambda v: lax.ppermute(v, 'fsdp', across)  4.57 us
    ppermute x1, starting transfers between devices, on_device(): lax.ppermute(v, 'replica', [(i, i ^ 1) for i in range(replicas)])  3.45 us
  transfers between devices with their start and end apart: 15, of which 7 were waited for; matrix products, arithmetic and copies ran while one was open for 0% of the time, Pallas kernels for 12%

profile of v5, /device:TPU:1, one launch (start us, length us, event | category | flops | bytes accessed | tf_op | source)
XLA Modules:
  0.0 114.1 jit_solution(3738091256205870318)
XLA Ops:
  0.6 4.3 %shard_map.77 = (f32[768,512]{1,0:T(8,128)}, f32[256,512]{1,0:T(8,128)}, f32[256,512]{1,0:T(8,128)}) custom-call(bf16[640,4096]{1,0:T(8,128)(2,1)} %tokens_ref.7, bf16[640,512]{1,0:T(8,128)(2,1)} %cot_ref.7), custom_call_target="tpu_custom_call" | custom-call | flops 1 | bytes 1 | tf_op jit(solution)/shard_map/pallas_call | solution.py:76
  4.9 2.1 %collective-permute-start.6 = (f32[768,512]{1,0:T(8,128)}, f32[768,512]{1,0:T(8,128)S(1)}, u32[]{:S(2)}, u32[]{:S(2)}) collective-permute-start(f32[768,512]{1,0:T(8,128)} %get-tuple-element.44), channel_id=1, source_target_pairs={{0,4},{1,5},{2,6},{3,7},{4,0},{5,1},{6,2},{7,3},{8,12},{9,13},{10,... | collective-permute-start | bytes 4718600 | tf_op jit(solution)/shard_map/ppermute | solution.py:335
  7.1 2.7 %collective-permute-start.1 = (f32[256,512]{1,0:T(8,128)}, f32[256,512]{1,0:T(8,128)S(1)}, u32[]{:S(2)}, u32[]{:S(2)}) collective-permute-start(f32[256,512]{1,0:T(8,128)} %get-tuple-element.36), channel_id=1, source_target_pairs={{0,3},{1,0},{2,1},{3,2},{4,7},{5,4},{6,5},{7,6},{8,11},{9,8},{10,9... | collective-permute-start | bytes 1572872 | tf_op jit(solution)/shard_map/ppermute | solution.py:334
  9.8 2.8 %shard_map.78 = (f32[256,512]{1,0:T(8,128)}, f32[256,512]{1,0:T(8,128)}) custom-call(bf16[640,4096]{1,0:T(8,128)(2,1)} %tokens_ref.7, bf16[640,512]{1,0:T(8,128)(2,1)} %cot_ref.7, f32[256,512]{1,0:T(8,128)} %get-tuple-element.32.refs_0_), custom_call_target="tpu_custom_call" | custom-call | flops 1 | bytes 1 | tf_op jit(solution)/shard_map/pallas_call | solution.py:76
  12.6 2.8 %collective-permute-start.4 = (f32[256,512]{1,0:T(8,128)}, f32[256,512]{1,0:T(8,128)S(1)}, u32[]{:S(2)}, u32[]{:S(2)}) collective-permute-start(f32[256,512]{1,0:T(8,128)} %get-tuple-element.42), channel_id=1, source_target_pairs={{0,3},{1,0},{2,1},{3,2},{4,7},{5,4},{6,5},{7,6},{8,11},{9,8},{10,9... | collective-permute-start | bytes 1572872 | tf_op jit(solution)/shard_map/ppermute | solution.py:334
  15.3 1.1 copy-done.2
  16.4 2.0 %shard_map.79 = (f32[256,512]{1,0:T(8,128)S(1)}, f32[256,512]{1,0:T(8,128)S(1)}) custom-call(bf16[640,4096]{1,0:T(8,128)(2,1)} %tokens_ref.7, bf16[640,512]{1,0:T(8,128)(2,1)} %cot_ref.7, f32[256,512]{1,0:T(8,128)S(1)} %copy-done.2), custom_call_target="tpu_custom_call" | custom-call | flops 1 | bytes 1 | tf_op jit(solution)/shard_map/pallas_call | solution.py:76
  18.4 1.7 %shard_map.80 = (f32[8,8,512]{2,1,0:T(8,128)S(1)}, f32[32,8,128]{2,1,0:T(8,128)S(1)}) custom-call(s32[32,8,4096]{2,1,0:T(8,128)} %index_ref.1, f32[256,512]{1,0:T(8,128)S(1)} %get-tuple-element.34.refs_0_), custom_call_target="tpu_custom_call" | custom-call | flops 1 | bytes 1 | tf_op jit(solution)/shard_map/pallas_call | solution.py:160
  20.1 0.3 collective-permute-done.1.refs_3_
  20.4 3.0 %collective-permute-done.refs_1_ = f32[256,512]{1,0:T(8,128)S(1)} collective-permute-done((f32[256,512]{1,0:T(8,128)}, f32[256,512]{1,0:T(8,128)S(1)}, u32[]{:S(2)}, u32[]{:S(2)}) %collective-permute-start) | collective-permute-done | bytes 524320 | tf_op jit(solution)/shard_map/ppermute | solution.py:333
  23.5 0.4 collective-permute-start.3
  23.9 1.2 %collective-permute-start.5 = (f32[256,512]{1,0:T(8,128)S(1)}, f32[256,512]{1,0:T(8,128)S(1)}, u32[]{:S(2)}, u32[]{:S(2)}) collective-permute-start(f32[256,512]{1,0:T(8,128)S(1)} %get-tuple-element.38.refs_0_), channel_id=1, source_target_pairs={{0,1},{1,2},{2,3},{3,0},{4,5},{5,6},{6,7},{7,4},{8,9},{9,10},{10,1... | collective-permute-start | bytes 1572872 | tf_op jit(solution)/shard_map/ppermute | solution.py:333
  25.0 4.0 %shard_map.82 = (f32[256,512]{1,0:T(8,128)S(1)}, f32[256,512]{1,0:T(8,128)S(1)}, f32[256,512]{1,0:T(8,128)S(1)}, f32[256,512]{1,0:T(8,128)S(1)}, f32[256,512]{1,...) custom-call(bf16[640,4096]{1,0:T(8,128)(2,1)} %tokens_ref.7, bf16[640,512]{1,0:T(8,128)(2,1)S(1)} %copy-done, ...), custom_call_target="tpu_custom_call" | custom-call | flops 1 | bytes 1 | tf_op jit(solution)/shard_map/pallas_call | solution.py:76
  29.0 11.1 %collective-permute-done.6.refs_1_ = f32[768,512]{1,0:T(8,128)S(1)} collective-permute-done((f32[768,512]{1,0:T(8,128)}, f32[768,512]{1,0:T(8,128)S(1)}, u32[]{:S(2)}, u32[]{:S(2)}) %collective-permute-start.6) | collective-permute-done | bytes 1572896 | tf_op jit(solution)/shard_map/ppermute | solution.py:335
  40.1 2.1 %collective-permute-start.9 = (f32[256,512]{1,0:T(8,128)S(1)}, f32[256,512]{1,0:T(8,128)S(1)}, u32[]{:S(2)}, u32[]{:S(2)}) collective-permute-start(f32[256,512]{1,0:T(8,128)S(1)} %get-tuple-element.51), channel_id=1, source_target_pairs={{0,4},{1,5},{2,6},{3,7},{4,0},{5,1},{6,2},{7,3},{8,12},{9,13},{10,... | collective-permute-start | bytes 1572872 | tf_op jit(solution)/shard_map/ppermute | solution.py:335
  42.3 1.7 %collective-permute-start.10 = (f32[128,512]{1,0:T(8,128)S(1)}, f32[128,512]{1,0:T(8,128)S(1)}, u32[]{:S(2)}, u32[]{:S(2)}) collective-permute-start(f32[128,512]{1,0:T(8,128)S(1)} %get-tuple-element.45.refs_6_), channel_id=1, source_target_pairs={{0,1},{1,2},{2,3},{3,0},{4,5},{5,6},{6,7},{7,4},{8,9},{9,10},{10,1... | collective-permute-start | bytes 786440 | tf_op jit(solution)/shard_map/ppermute | solution.py:333
  44.0 1.9 %collective-permute-done.5.refs_5_ = f32[256,512]{1,0:T(8,128)S(1)} collective-permute-done((f32[256,512]{1,0:T(8,128)S(1)}, f32[256,512]{1,0:T(8,128)S(1)}, u32[]{:S(2)}, u32[]{:S(2)}) %collective-permute-start.5) | collective-permute-done | bytes 524320 | tf_op jit(solution)/shard_map/ppermute | solution.py:333
  46.0 0.3 collective-permute-start.7
  46.4 0.3 collective-permute-start.8
  46.7 5.2 %collective-permute-done.10.refs_2_ = f32[128,512]{1,0:T(8,128)S(1)} collective-permute-done((f32[128,512]{1,0:T(8,128)S(1)}, f32[128,512]{1,0:T(8,128)S(1)}, u32[]{:S(2)}, u32[]{:S(2)}) %collective-permute-start.10) | collective-permute-done | bytes 262176 | tf_op jit(solution)/shard_map/ppermute | solution.py:333
  52.1 2.7 %collective-permute-start.12 = (f32[128,512]{1,0:T(8,128)S(1)}, f32[128,512]{1,0:T(8,128)S(1)}, u32[]{:S(2)}, u32[]{:S(2)}) collective-permute-start(f32[128,512]{1,0:T(8,128)S(1)} %shard_map.85.refs_3_), channel_id=1, source_target_pairs={{0,3},{1,0},{2,1},{3,2},{4,7},{5,4},{6,5},{7,6},{8,11},{9,8},{10,9... | collective-permute-start | bytes 786440 | tf_op jit(solution)/shard_map/ppermute | solution.py:334
  54.9 1.3 %collective-permute-start.13 = (f32[128,512]{1,0:T(8,128)S(1)}, f32[128,512]{1,0:T(8,128)S(1)}, u32[]{:S(2)}, u32[]{:S(2)}) collective-permute-start(f32[128,512]{1,0:T(8,128)S(1)} %get-tuple-element.55), channel_id=1, source_target_pairs={{0,3},{1,0},{2,1},{3,2},{4,7},{5,4},{6,5},{7,6},{8,11},{9,8},{10,9... | collective-permute-start | bytes 786440 | tf_op jit(solution)/shard_map/ppermute | solution.py:334
  56.1 7.5 %collective-permute-done.7.refs_1_ = f32[256,512]{1,0:T(8,128)S(1)} collective-permute-done((f32[256,512]{1,0:T(8,128)S(1)}, f32[256,512]{1,0:T(8,128)S(1)}, u32[]{:S(2)}, u32[]{:S(2)}) %collective-permute-start.7) | collective-permute-done | bytes 524320 | tf_op jit(solution)/shard_map/ppermute | solution.py:335
  63.6 0.9 shard_map.88
  64.5 1.0 collective-permute-done.13.refs_3_
  65.5 0.9 shard_map.89
  66.4 23.8 %all_to_all.10.value_ref = f32[32,8,128]{2,1,0:T(8,128)S(1)} all-to-all(f32[32,8,128]{2,1,0:T(8,128)S(1)} %get-tuple-element.60), channel_id=1, replica_groups=mesh['replica'=32,'fsdp'=8] {'replica'}, dimensions={0} | all-to-all | bytes 262144 | tf_op jit(solution)/shard_map/all_to_all | solution.py:380
  90.2 0.6 shard_map.90
  90.8 16.8 %all_to_all.11.refs_5_.mine_ref = f32[16,64,128]{2,1,0:T(8,128)S(1)} all-to-all(f32[16,64,128]{2,1,0:T(8,128)S(1)} %shard_map.90), channel_id=1, replica_groups={{0,16,32,48,64,80,96,112,128,144,160,176,192,208,224,240},{8,24,40,56,7..., dimensions={0} | all-to-all | bytes 1048576 | tf_op jit(solution)/shard_map/all_to_all | solution.py:383
  107.6 3.5 %collective-permute-start.14 = (f32[16,64,128]{2,1,0:T(8,128)S(1)}, f32[16,64,128]{2,1,0:T(8,128)S(1)}, u32[]{:S(2)}, u32[]{:S(2)}) collective-permute-start(f32[16,64,128]{2,1,0:T(8,128)S(1)} %all_to_all.11.refs_5_.mine_ref), channel_id=1, source_target_pairs={{0,8},{8,0},{16,24},{24,16},{32,40},{40,32},{48,56},{56,48},{64,72... | collective-permute-start | bytes 1572872 | tf_op jit(solution)/shard_map/ppermute | solution.py:336
  111.0 1.6 %shard_map.91 = f32[512,512]{1,0:T(8,128)} custom-call(f32[256,512]{1,0:T(8,128)S(1)} %get-tuple-element.54.refs_0_, f32[256,512]{1,0:T(8,128)S(1)} %get-tuple-element.57.refs_1_, f32[512,256]{1,0:T(8,128)S(1)} %get-tuple-element.58.refs_2_, f32[512,256]{1,0:T(8,128)S(1)} %get-tuple-element.59.refs_3_, bf16[384,128]{1,0:T(8,128)(2,1)S(1)} %copy-done.4, ...), custom_call_target="tpu_custom_call" | custom-call | flops 1 | bytes 1 | tf_op jit(solution)/shard_map/pallas_call | solution.py:254
  112.6 1.3 %shard_map.92 = f32[512,512]{1,0:T(8,128)} custom-call(f32[16,64,128]{2,1,0:T(8,128)S(1)} %all_to_all.11.refs_5_.mine_ref, f32[16,64,128]{2,1,0:T(8,128)S(1)} %collective-permute-done.14.other_ref, bf16[384,128]{1,0:T(8,128)(2,1)S(1)} %copy-done.4), custom_call_target="tpu_custom_call" | custom-call | flops 1 | bytes 1 | tf_op jit(solution)/shard_map/pallas_call | solution.py:312
  (26 shorter events, 0.6 us)
Async XLA Ops:
  4.9 35.2 %collective-permute-start.6 = (f32[768,512]{1,0:T(8,128)}, f32[768,512]{1,0:T(8,128)S(1)}, u32[]{:S(2)}, u32[]{:S(2)}) collective-permute-start(f32[768,512]{1,0:T(8,128)} %get-tuple-element.44), channel_id=1, source_target_pairs={{0,4},{1,5},{2,6},{3,7},{4,0},{5,1},{6,2},{7,3},{8,12},{9,13},{10,... | collective-permute-start | bytes 4718600 | tf_op jit(solution)/shard_map/ppermute | solution.py:335
  7.1 13.3 %collective-permute-start.1 = (f32[256,512]{1,0:T(8,128)}, f32[256,512]{1,0:T(8,128)S(1)}, u32[]{:S(2)}, u32[]{:S(2)}) collective-permute-start(f32[256,512]{1,0:T(8,128)} %get-tuple-element.36), channel_id=1, source_target_pairs={{0,3},{1,0},{2,1},{3,2},{4,7},{5,4},{6,5},{7,6},{8,11},{9,8},{10,9... | collective-permute-start | bytes 1572872 | tf_op jit(solution)/shard_map/ppermute | solution.py:334
  9.8 13.6 %collective-permute-start = (f32[256,512]{1,0:T(8,128)}, f32[256,512]{1,0:T(8,128)S(1)}, u32[]{:S(2)}, u32[]{:S(2)}) collective-permute-start(f32[256,512]{1,0:T(8,128)} %get-tuple-element.32.refs_0_), channel_id=1, source_target_pairs={{0,1},{1,2},{2,3},{3,0},{4,5},{5,6},{6,7},{7,4},{8,9},{9,10},{10,1... | collective-permute-start | bytes 1572872 | tf_op jit(solution)/shard_map/ppermute | solution.py:333
  12.6 29.7 %collective-permute-start.4 = (f32[256,512]{1,0:T(8,128)}, f32[256,512]{1,0:T(8,128)S(1)}, u32[]{:S(2)}, u32[]{:S(2)}) collective-permute-start(f32[256,512]{1,0:T(8,128)} %get-tuple-element.42), channel_id=1, source_target_pairs={{0,3},{1,0},{2,1},{3,2},{4,7},{5,4},{6,5},{7,6},{8,11},{9,8},{10,9... | collective-permute-start | bytes 1572872 | tf_op jit(solution)/shard_map/ppermute | solution.py:334
  15.3 28.6 %collective-permute-start.2 = (f32[256,512]{1,0:T(8,128)}, f32[256,512]{1,0:T(8,128)S(1)}, u32[]{:S(2)}, u32[]{:S(2)}) collective-permute-start(f32[256,512]{1,0:T(8,128)} %get-tuple-element.33.refs_0_), channel_id=1, source_target_pairs={{0,1},{1,2},{2,3},{3,0},{4,5},{5,6},{6,7},{7,4},{8,9},{9,10},{10,1... | collective-permute-start | bytes 1572872 | tf_op jit(solution)/shard_map/ppermute | solution.py:333
  15.3 1.1 copy-start.2
  18.4 6.6 %copy-start = (bf16[640,512]{1,0:T(8,128)(2,1)S(1)}, bf16[640,512]{1,0:T(8,128)(2,1)}, u32[]{:S(2)}) copy-start(bf16[640,512]{1,0:T(8,128)(2,1)} %cot_ref.7) | copy-start | bytes 1966084
  23.5 20.5 %collective-permute-start.3 = (f32[256,512]{1,0:T(8,128)S(1)}, f32[256,512]{1,0:T(8,128)S(1)}, u32[]{:S(2)}, u32[]{:S(2)}) collective-permute-start(f32[256,512]{1,0:T(8,128)S(1)} %get-tuple-element.40), channel_id=1, source_target_pairs={{0,3},{1,0},{2,1},{3,2},{4,7},{5,4},{6,5},{7,6},{8,11},{9,8},{10,9... | collective-permute-start | bytes 1572872 | tf_op jit(solution)/shard_map/ppermute | solution.py:334
  23.9 22.0 %collective-permute-start.5 = (f32[256,512]{1,0:T(8,128)S(1)}, f32[256,512]{1,0:T(8,128)S(1)}, u32[]{:S(2)}, u32[]{:S(2)}) collective-permute-start(f32[256,512]{1,0:T(8,128)S(1)} %get-tuple-element.38.refs_0_), channel_id=1, source_target_pairs={{0,1},{1,2},{2,3},{3,0},{4,5},{5,6},{6,7},{7,4},{8,9},{9,10},{10,1... | collective-permute-start | bytes 1572872 | tf_op jit(solution)/shard_map/ppermute | solution.py:333
  40.1 14.6 %collective-permute-start.9 = (f32[256,512]{1,0:T(8,128)S(1)}, f32[256,512]{1,0:T(8,128)S(1)}, u32[]{:S(2)}, u32[]{:S(2)}) collective-permute-start(f32[256,512]{1,0:T(8,128)S(1)} %get-tuple-element.51), channel_id=1, source_target_pairs={{0,4},{1,5},{2,6},{3,7},{4,0},{5,1},{6,2},{7,3},{8,12},{9,13},{10,... | collective-permute-start | bytes 1572872 | tf_op jit(solution)/shard_map/ppermute | solution.py:335
  42.3 9.6 %collective-permute-start.10 = (f32[128,512]{1,0:T(8,128)S(1)}, f32[128,512]{1,0:T(8,128)S(1)}, u32[]{:S(2)}, u32[]{:S(2)}) collective-permute-start(f32[128,512]{1,0:T(8,128)S(1)} %get-tuple-element.45.refs_6_), channel_id=1, source_target_pairs={{0,1},{1,2},{2,3},{3,0},{4,5},{5,6},{6,7},{7,4},{8,9},{9,10},{10,1... | collective-permute-start | bytes 786440 | tf_op jit(solution)/shard_map/ppermute | solution.py:333
  46.0 17.6 %collective-permute-start.7 = (f32[256,512]{1,0:T(8,128)S(1)}, f32[256,512]{1,0:T(8,128)S(1)}, u32[]{:S(2)}, u32[]{:S(2)}) collective-permute-start(f32[256,512]{1,0:T(8,128)S(1)} %get-tuple-element.47.refs_2_), channel_id=1, source_target_pairs={{0,4},{1,5},{2,6},{3,7},{4,0},{5,1},{6,2},{7,3},{8,12},{9,13},{10,... | collective-permute-start | bytes 1572872 | tf_op jit(solution)/shard_map/ppermute | solution.py:335
  46.4 8.4 %collective-permute-start.8 = (f32[128,512]{1,0:T(8,128)S(1)}, f32[128,512]{1,0:T(8,128)S(1)}, u32[]{:S(2)}, u32[]{:S(2)}) collective-permute-start(f32[128,512]{1,0:T(8,128)S(1)} %get-tuple-element.49), channel_id=1, source_target_pairs={{0,3},{1,0},{2,1},{3,2},{4,7},{5,4},{6,5},{7,6},{8,11},{9,8},{10,9... | collective-permute-start | bytes 786440 | tf_op jit(solution)/shard_map/ppermute | solution.py:334
  46.7 16.9 %copy-start.1 = (f32[1,512,512]{2,1,0:T(8,128)S(1)}, f32[1,512,512]{2,1,0:T(8,128)}, u32[]{:S(2)}) copy-start(f32[1,512,512]{2,1,0:T(8,128)} %param.8) | copy-start | bytes 3145732
  46.7 16.9 %copy-start.3 = (bf16[128,384]{1,0:T(8,128)(2,1)S(1)}, bf16[128,384]{1,0:T(8,128)(2,1)}, u32[]{:S(2)}) copy-start(bf16[128,384]{1,0:T(8,128)(2,1)} %constant.4.clone.refs_4_.refs_6_) | copy-start | bytes 294916
  52.0 13.5 %collective-permute-start.11 = (f32[256,512]{1,0:T(8,128)S(1)}, f32[256,512]{1,0:T(8,128)S(1)}, u32[]{:S(2)}, u32[]{:S(2)}) collective-permute-start(f32[256,512]{1,0:T(8,128)S(1)} %shard_map.86.refs_5_), channel_id=1, source_target_pairs={{0,1},{1,2},{2,3},{3,0},{4,5},{5,6},{6,7},{7,4},{8,9},{9,10},{10,1... | collective-permute-start | bytes 1572872 | tf_op jit(solution)/shard_map/ppermute | solution.py:333
  52.1 12.4 %collective-permute-start.12 = (f32[128,512]{1,0:T(8,128)S(1)}, f32[128,512]{1,0:T(8,128)S(1)}, u32[]{:S(2)}, u32[]{:S(2)}) collective-permute-start(f32[128,512]{1,0:T(8,128)S(1)} %shard_map.85.refs_3_), channel_id=1, source_target_pairs={{0,3},{1,0},{2,1},{3,2},{4,7},{5,4},{6,5},{7,6},{8,11},{9,8},{10,9... | collective-permute-start | bytes 786440 | tf_op jit(solution)/shard_map/ppermute | solution.py:334
  54.8 56.2 %copy-start.4 = (bf16[384,128]{1,0:T(8,128)(2,1)S(1)}, bf16[384,128]{1,0:T(8,128)(2,1)}, u32[]{:S(2)}) copy-start(bf16[384,128]{1,0:T(8,128)(2,1)} %constant.5.clone.refs_4_.cos_ref) | copy-start | bytes 294916
  54.9 10.6 %collective-permute-start.13 = (f32[128,512]{1,0:T(8,128)S(1)}, f32[128,512]{1,0:T(8,128)S(1)}, u32[]{:S(2)}, u32[]{:S(2)}) collective-permute-start(f32[128,512]{1,0:T(8,128)S(1)} %get-tuple-element.55), channel_id=1, source_target_pairs={{0,3},{1,0},{2,1},{3,2},{4,7},{5,4},{6,5},{7,6},{8,11},{9,8},{10,9... | collective-permute-start | bytes 786440 | tf_op jit(solution)/shard_map/ppermute | solution.py:334
  107.6 5.0 %collective-permute-start.14 = (f32[16,64,128]{2,1,0:T(8,128)S(1)}, f32[16,64,128]{2,1,0:T(8,128)S(1)}, u32[]{:S(2)}, u32[]{:S(2)}) collective-permute-start(f32[16,64,128]{2,1,0:T(8,128)S(1)} %all_to_all.11.refs_5_.mine_ref), channel_id=1, source_target_pairs={{0,8},{8,0},{16,24},{24,16},{32,40},{40,32},{48,56},{56,48},{64,72... | collective-permute-start | bytes 1572872 | tf_op jit(solution)/shard_map/ppermute | solution.py:336
